TPU v7x, 256 devices: a whole 4x4x8 slice. The times are simulated.
256 devices in a mesh: gx: 4 (over x), gy: 8 (over z_lo, core), gz: 8 (over y, z_hi).
Axes of the slice: x: 4, y: 4, z: 8 (z_hi: 2, z_lo: 4; z = z_hi * 4 + z_lo), core: 2. Of those that a mesh axis runs over, the one named last changes fastest.
Arguments:
- source: float32 [64, 256, 1024], P('gx', 'gy', 'gz'), may hold values from -8 to 8
- conductivity: float32 [64, 256, 1024], P('gx', 'gy', 'gz'), may hold values from 0.1 to 10
Outputs:
- correction: float32 [64, 256, 1024], P('gx', 'gy', 'gz')
- residual: float32 [64, 256, 1024], P('gx', 'gy', 'gz')
All inputs are finite; a program needn't handle non-finite values.
Results may differ from a plain program's by a relative error of at most 0.0001.
Values sent between devices are 32-bit elements; how exact they have to be, the bound alone decides.
A program may use at most 128 MiB of HBM per device.

v0:
```python
import jax
import jax.numpy as jnp
from jax import lax
from jax.sharding import PartitionSpec as P

CHEB_HIGH = 2.0
CHEB_LOW = 0.3


def padded_2(block, sides, width):
    for axis, dim in sides:
        count = lax.axis_size(axis)
        forward = [(i, i + 1) for i in range(count - 1)]
        backward = [(target, source) for source, target in forward]
        low = lax.ppermute(
            lax.slice_in_dim(block, block.shape[dim] - width, None, axis=dim), axis, forward
        )
        high = lax.ppermute(lax.slice_in_dim(block, 0, width, axis=dim), axis, backward)
        block = jnp.concatenate([low, block, high], axis=dim)
    return block


def restrict_sum(field):
    size_x, size_y, size_z = field.shape
    return field.reshape(size_x // 2, 2, size_y // 2, 2, size_z // 2, 2).sum(axis=(1, 3, 5))


def coarsen_mean(field):
    return restrict_sum(field) * 0.125


def prolong(field):
    return jnp.repeat(jnp.repeat(jnp.repeat(field, 2, axis=0), 2, axis=1), 2, axis=2)


def level_couplings(padded, coeff, factor):
    parts = (
        padded[:-2, 1:-1, 1:-1],
        padded[2:, 1:-1, 1:-1],
        padded[1:-1, :-2, 1:-1],
        padded[1:-1, 2:, 1:-1],
        padded[1:-1, 1:-1, :-2],
        padded[1:-1, 1:-1, 2:],
    )
    couplings = tuple((factor * 0.5 * (coeff + neighbour) for neighbour in parts))
    diagonal = couplings[0]
    for extra in couplings[1:]:
        diagonal = diagonal + extra
    return (couplings, diagonal)


def apply_op(padded, field, couplings, diagonal):
    parts = (
        padded[:-2, 1:-1, 1:-1],
        padded[2:, 1:-1, 1:-1],
        padded[1:-1, :-2, 1:-1],
        padded[1:-1, 2:, 1:-1],
        padded[1:-1, 1:-1, :-2],
        padded[1:-1, 1:-1, 2:],
    )
    neighbours = couplings[0] * parts[0]
    for index in range(1, 6):
        neighbours = neighbours + couplings[index] * parts[index]
    return diagonal * field - neighbours


def smooth(target, start, operators, sweeps, extend):
    couplings, diagonal = operators
    centre = (CHEB_HIGH + CHEB_LOW) / 2.0
    half_width = (CHEB_HIGH - CHEB_LOW) / 2.0
    sharpness = centre / half_width
    weight = 1.0 / sharpness
    if start is None:
        update = target / diagonal * (1.0 / centre)
        approx = update
    else:
        remain = target - apply_op(extend(start), start, couplings, diagonal)
        update = remain / diagonal * (1.0 / centre)
        approx = start + update
    for sweep in range(sweeps - 1):
        remain = target - apply_op(extend(approx), approx, couplings, diagonal)
        weight_new = 1.0 / (2.0 * sharpness - weight)
        update = weight_new * weight * update + 2.0 * weight_new / half_width * (remain / diagonal)
        approx = approx + update
        weight = weight_new
    return approx


def vcycle(target, coeff, extend):
    coeff_low = coarsen_mean(coeff)
    upper = level_couplings(extend(coeff), coeff, 8.0)
    lower = level_couplings(extend(coeff_low), coeff_low, 16.0)
    approx = smooth(target, None, upper, 2, extend)
    residue = target - apply_op(extend(approx), approx, upper[0], upper[1])
    lower_fix = smooth(restrict_sum(residue), None, lower, 4, extend)
    approx = approx + prolong(lower_fix)
    return smooth(target, approx, upper, 2, extend)


def fine_extend(field):
    return padded_2(field, (("gx", 0), ("gy", 1), ("gz", 2)), 1)


def middle_extend(field):
    return padded_2(field, (("gx", 0), ("gy", 1), ("gz", 2)), 1)


def coarse_extend(field):
    return padded_2(field, (("gx", 0), ("gy", 1), ("gz", 2)), 1)


def shards(source, conductivity):
    targets = [source]
    coeffs = [conductivity]
    for level in range(3):
        targets.append(restrict_sum(targets[-1]))
        coeffs.append(coarsen_mean(coeffs[-1]))
    extenders = [fine_extend, middle_extend, middle_extend]
    corrections = []
    fine_ops = None
    for level in range(3):
        extend = extenders[level]
        operators = level_couplings(extend(coeffs[level]), coeffs[level], float(2**level))
        if level == 0:
            fine_ops = operators
        first = smooth(targets[level], None, operators, 3, extend)
        corrections.append(smooth(targets[level], first, operators, 3, extend))
    summed = vcycle(targets[3], coeffs[3], coarse_extend)
    for level in (2, 1, 0):
        summed = corrections[level] + prolong(summed)
    residual = source - apply_op(fine_extend(summed), summed, fine_ops[0], fine_ops[1])
    return (summed, residual)


def solution(mesh):
    in_specs = (P("gx", "gy", "gz"), P("gx", "gy", "gz"))
    out_specs = (P("gx", "gy", "gz"), P("gx", "gy", "gz"))
    return jax.shard_map(shards, mesh=mesh, in_specs=in_specs, out_specs=out_specs, check_vma=False)
```

profile of v0, /device:TPU:31, one launch (start us, length us, event | category | flops | bytes accessed | tf_op | source)
XLA Modules:
  0.0 923.4 jit_solution(9733321176790906742)
XLA Ops:
  0.6 18.9 %reshape.75 = f32[8,2,16,2,64,2]{5,4,3,2,1,0:T(8,128)} reshape(f32[16,32,128]{2,1,0:T(8,128)} %param.3) | data formatting | bytes 524288 | tf_op jit(solution)/shard_map/reshape | solution.py:25
  19.5 7.0 reduce_sum.89
  42.5 18.1 %reshape.74 = f32[8,2,16,2,64,2]{5,4,3,2,1,0:T(8,128)} reshape(f32[16,32,128]{2,1,0:T(8,128)S(1)} %copy-done.1) | data formatting | bytes 524288 | tf_op jit(solution)/shard_map/reshape | solution.py:25
  60.6 7.0 reduce_sum.88
  72.9 5.5 collective-permute-start.110
  83.5 7.9 collective-permute-start.112
  122.4 5.7 collective-permute-start.118
  144.7 6.0 collective-permute-start.122
  204.7 6.4 collective-permute-start.137
  214.0 6.3 collective-permute-done.136
  238.1 7.2 collective-permute-start.142
  255.9 6.4 collective-permute-start.146
  263.1 6.1 collective-permute-start.149
  272.3 6.1 collective-permute-done.148
  286.6 7.0 collective-permute-start.152
  300.0 5.9 collective-permute-start.154
  320.3 5.6 collective-permute-start.83
  355.2 7.1 collective-permute-start.89
  395.5 7.0 collective-permute-start.95
  422.5 7.1 collective-permute-start.41
  436.8 8.0 collective-permute-start.101
  466.2 8.4 collective-permute-start.107
  481.0 7.3 collective-permute-start.47
  493.7 11.3 %collective-permute-done.46 = f32[10,18,1]{2,1,0:T(8,128)S(1)} collective-permute-done((f32[10,18,1]{2,1,0:T(8,128)S(1)}, f32[10,18,1]{2,1,0:T(8,128)S(1)}, u32[]{:S(2)}, u32[]{:S(2)}) %collective-permute-start.46) | collective-permute-done | bytes 752 | tf_op jit(solution)/shard_map/ppermute | solution.py:15
  535.6 8.2 collective-permute-start.5
  545.1 18.8 %collective-permute-done.4 = f32[18,34,1]{2,1,0:T(8,128)S(1)} collective-permute-done((f32[18,34,1]{2,1,0:T(8,128)S(1)}, f32[18,34,1]{2,1,0:T(8,128)S(1)}, u32[]{:S(2)}, u32[]{:S(2)}) %collective-permute-start.4) | collective-permute-done | bytes 2480 | tf_op jit(solution)/shard_map/ppermute | solution.py:15
  564.3 5.7 collective-permute-start.7
  590.8 8.9 collective-permute-start.11
  601.7 13.8 %collective-permute-done.11 = f32[18,34,1]{2,1,0:T(8,128)S(1)} collective-permute-done((f32[18,34,1]{2,1,0:T(8,128)S(1)}, f32[18,34,1]{2,1,0:T(8,128)S(1)}, u32[]{:S(2)}, u32[]{:S(2)}) %collective-permute-start.11) | collective-permute-done | bytes 2480 | tf_op jit(solution)/shard_map/ppermute | solution.py:18
  615.5 9.2 collective-permute-done.10
  630.8 6.3 collective-permute-start.59
  643.1 7.0 collective-permute-start.14
  652.8 5.7 collective-permute-start.17
  667.9 10.9 %collective-permute-done.16 = f32[18,34,1]{2,1,0:T(8,128)S(1)} collective-permute-done((f32[18,34,1]{2,1,0:T(8,128)S(1)}, f32[18,34,1]{2,1,0:T(8,128)S(1)}, u32[]{:S(2)}, u32[]{:S(2)}) %collective-permute-start.16) | collective-permute-done | bytes 2480 | tf_op jit(solution)/shard_map/ppermute | solution.py:15
  687.1 20.8 %collective-permute-start.62 = (f32[10,1,64]{2,1,0:T(1,128)S(1)}, f32[10,1,64]{2,1,0:T(1,128)S(1)}, u32[]{:S(2)}, u32[]{:S(2)}) collective-permute-start(f32[10,1,64]{2,1,0:T(1,128)S(1)} %get-tuple-element.117), channel_id=1, source_target_pairs={{0,8},{8,16},{16,24},{24,32},{32,40},{40,48},{48,56},{1,9},{9,17},... | collective-permute-start | bytes 7688 | tf_op jit(solution)/shard_map/ppermute | solution.py:15
  714.5 6.2 collective-permute-start.23
  723.8 7.0 collective-permute-start.65
  733.8 13.4 %collective-permute-done.22 = f32[18,34,1]{2,1,0:T(8,128)S(1)} collective-permute-done((f32[18,34,1]{2,1,0:T(8,128)S(1)}, f32[18,34,1]{2,1,0:T(8,128)S(1)}, u32[]{:S(2)}, u32[]{:S(2)}) %collective-permute-start.22) | collective-permute-done | bytes 2480 | tf_op jit(solution)/shard_map/ppermute | solution.py:15
  759.8 11.9 %collective-permute-start.26 = (f32[18,1,128]{2,1,0:T(1,128)S(1)}, f32[18,1,128]{2,1,0:T(1,128)S(1)}, u32[]{:S(2)}, u32[]{:S(2)}) collective-permute-start(f32[18,1,128]{2,1,0:T(1,128)S(1)} %get-tuple-element.79), channel_id=1, source_target_pairs={{0,8},{8,16},{16,24},{24,32},{32,40},{40,48},{48,56},{1,9},{9,17},... | collective-permute-start | bytes 27656 | tf_op jit(solution)/shard_map/ppermute | solution.py:15
  777.6 6.8 collective-permute-start.28
  791.5 18.2 %collective-permute-done.28 = f32[18,34,1]{2,1,0:T(8,128)S(1)} collective-permute-done((f32[18,34,1]{2,1,0:T(8,128)S(1)}, f32[18,34,1]{2,1,0:T(8,128)S(1)}, u32[]{:S(2)}, u32[]{:S(2)}) %collective-permute-start.28) | collective-permute-done | bytes 2480 | tf_op jit(solution)/shard_map/ppermute | solution.py:15
  827.3 7.3 collective-permute-start.70
  838.4 7.1 collective-permute-start.34
  851.4 11.4 %collective-permute-done.34 = f32[18,34,1]{2,1,0:T(8,128)} collective-permute-done((f32[18,34,1]{2,1,0:T(8,128)}, f32[18,34,1]{2,1,0:T(8,128)}, u32[]{:S(2)}, u32[]{:S(2)}) %collective-permute-start.34) | collective-permute-done | bytes 2480 | tf_op jit(solution)/shard_map/ppermute | solution.py:15
  871.5 12.2 %collective-permute-start.165 = (f32[18,1,128]{2,1,0:T(1,128)S(1)}, f32[18,1,128]{2,1,0:T(1,128)S(1)}, u32[]{:S(2)}, u32[]{:S(2)}) collective-permute-start(f32[18,1,128]{2,1,0:T(1,128)S(1)} %get-tuple-element.76), channel_id=1, source_target_pairs={{8,0},{16,8},{24,16},{32,24},{40,32},{48,40},{56,48},{9,1},{17,9},... | collective-permute-start | bytes 27656 | tf_op jit(solution)/shard_map/ppermute | solution.py:18
  889.8 7.3 collective-permute-start.166
  897.1 7.1 collective-permute-done.167
  904.2 18.1 %collective-permute-done.166 = f32[18,34,1]{2,1,0:T(8,128)S(1)} collective-permute-done((f32[18,34,1]{2,1,0:T(8,128)S(1)}, f32[18,34,1]{2,1,0:T(8,128)S(1)}, u32[]{:S(2)}, u32[]{:S(2)}) %collective-permute-start.166) | collective-permute-done | bytes 2480 | tf_op jit(solution)/shard_map/ppermute | solution.py:15
  (506 shorter events, 481.3 us)
Async XLA Ops:
  29.4 40.9 %collective-permute-start.127 = (f32[1,2,8]{2,1,0:T(2,128)S(1)}, f32[1,2,8]{2,1,0:T(2,128)S(1)}, u32[]{:S(2)}, u32[]{:S(2)}) collective-permute-start(f32[1,2,8]{2,1,0:T(2,128)S(1)} %multiply_bitcast_fusion), channel_id=1, source_target_pairs={{64,0},{128,64},{192,128},{65,1},{129,65},{193,129},{66,2},{130,66... | collective-permute-start | bytes 200 | tf_op jit(solution)/shard_map/ppermute | solution.py:18
  31.9 39.7 %collective-permute-start.126 = (f32[1,2,8]{2,1,0:T(2,128)S(1)}, f32[1,2,8]{2,1,0:T(2,128)S(1)}, u32[]{:S(2)}, u32[]{:S(2)}) collective-permute-start(f32[1,2,8]{2,1,0:T(2,128)S(1)} %multiply_bitcast_fusion), channel_id=1, source_target_pairs={{0,64},{64,128},{128,192},{1,65},{65,129},{129,193},{2,66},{66,130... | collective-permute-start | bytes 200 | tf_op jit(solution)/shard_map/ppermute | solution.py:15
  33.2 39.7 %collective-permute-start.108 = (f32[1,4,16]{2,1,0:T(4,128)S(1)}, f32[1,4,16]{2,1,0:T(4,128)S(1)}, u32[]{:S(2)}, u32[]{:S(2)}) collective-permute-start(f32[1,4,16]{2,1,0:T(4,128)S(1)} %get-tuple-element.226), channel_id=1, source_target_pairs={{0,64},{64,128},{128,192},{1,65},{65,129},{129,193},{2,66},{66,130... | collective-permute-start | bytes 776 | tf_op jit(solution)/shard_map/ppermute | solution.py:15
  34.5 38.4 %collective-permute-start.109 = (f32[1,4,16]{2,1,0:T(4,128)S(1)}, f32[1,4,16]{2,1,0:T(4,128)S(1)}, u32[]{:S(2)}, u32[]{:S(2)}) collective-permute-start(f32[1,4,16]{2,1,0:T(4,128)S(1)} %get-tuple-element.225), channel_id=1, source_target_pairs={{64,0},{128,64},{192,128},{65,1},{129,65},{193,129},{66,2},{130,66... | collective-permute-start | bytes 776 | tf_op jit(solution)/shard_map/ppermute | solution.py:18
  39.1 94.0 %collective-permute-start.73 = (f32[1,8,32]{2,1,0:T(8,128)S(1)}, f32[1,8,32]{2,1,0:T(8,128)S(1)}, u32[]{:S(2)}, u32[]{:S(2)}) collective-permute-start(f32[1,8,32]{2,1,0:T(8,128)S(1)} %get-tuple-element.186), channel_id=1, source_target_pairs={{64,0},{128,64},{192,128},{65,1},{129,65},{193,129},{66,2},{130,66... | collective-permute-start | bytes 3080 | tf_op jit(solution)/shard_map/ppermute | solution.py:18
  70.3 67.1 %collective-permute-start.72 = (f32[1,8,32]{2,1,0:T(8,128)S(1)}, f32[1,8,32]{2,1,0:T(8,128)S(1)}, u32[]{:S(2)}, u32[]{:S(2)}) collective-permute-start(f32[1,8,32]{2,1,0:T(8,128)S(1)} %get-tuple-element.185), channel_id=1, source_target_pairs={{0,64},{64,128},{128,192},{1,65},{65,129},{129,193},{2,66},{66,130... | collective-permute-start | bytes 3080 | tf_op jit(solution)/shard_map/ppermute | solution.py:15
  71.6 315.7 %collective-permute-start.36 = (f32[1,16,64]{2,1,0:T(8,128)S(1)}, f32[1,16,64]{2,1,0:T(8,128)S(1)}, u32[]{:S(2)}, u32[]{:S(2)}) collective-permute-start(f32[1,16,64]{2,1,0:T(8,128)S(1)} %get-tuple-element.138), channel_id=1, source_target_pairs={{0,64},{64,128},{128,192},{1,65},{65,129},{129,193},{2,66},{66,130... | collective-permute-start | bytes 12296 | tf_op jit(solution)/shard_map/ppermute | solution.py:15
  128.1 259.2 %collective-permute-start.37 = (f32[1,16,64]{2,1,0:T(8,128)S(1)}, f32[1,16,64]{2,1,0:T(8,128)S(1)}, u32[]{:S(2)}, u32[]{:S(2)}) collective-permute-start(f32[1,16,64]{2,1,0:T(8,128)S(1)} %get-tuple-element.137), channel_id=1, source_target_pairs={{64,0},{128,64},{192,128},{65,1},{129,65},{193,129},{66,2},{130,66... | collective-permute-start | bytes 12296 | tf_op jit(solution)/shard_map/ppermute | solution.py:18
  131.7 378.9 %collective-permute-start = (f32[1,32,128]{2,1,0:T(8,128)S(1)}, f32[1,32,128]{2,1,0:T(8,128)S(1)}, u32[]{:S(2)}, u32[]{:S(2)}) collective-permute-start(f32[1,32,128]{2,1,0:T(8,128)S(1)} %get-tuple-element.102), channel_id=1, source_target_pairs={{0,64},{64,128},{128,192},{1,65},{65,129},{129,193},{2,66},{66,130... | collective-permute-start | bytes 49160 | tf_op jit(solution)/shard_map/ppermute | solution.py:15
  378.3 132.5 %collective-permute-start.1 = (f32[1,32,128]{2,1,0:T(8,128)S(1)}, f32[1,32,128]{2,1,0:T(8,128)S(1)}, u32[]{:S(2)}, u32[]{:S(2)}) collective-permute-start(f32[1,32,128]{2,1,0:T(8,128)S(1)} %get-tuple-element.101), channel_id=1, source_target_pairs={{64,0},{128,64},{192,128},{65,1},{129,65},{193,129},{66,2},{130,66... | collective-permute-start | bytes 49160 | tf_op jit(solution)/shard_map/ppermute | solution.py:18
  414.5 15.1 %collective-permute-start.98 = (f32[6,1,32]{2,1,0:T(1,128)S(1)}, f32[6,1,32]{2,1,0:T(1,128)S(1)}, u32[]{:S(2)}, u32[]{:S(2)}) collective-permute-start(f32[6,1,32]{2,1,0:T(1,128)S(1)} %get-tuple-element.166), channel_id=1, source_target_pairs={{0,8},{8,16},{16,24},{24,32},{32,40},{40,48},{48,56},{1,9},{9,17},... | collective-permute-start | bytes 2312 | tf_op jit(solution)/shard_map/ppermute | solution.py:15
  419.5 17.3 %collective-permute-start.40 = (f32[10,18,1]{2,1,0:T(8,128)S(1)}, f32[10,18,1]{2,1,0:T(8,128)S(1)}, u32[]{:S(2)}, u32[]{:S(2)}) collective-permute-start(f32[10,18,1]{2,1,0:T(8,128)S(1)} %get-tuple-element.114), channel_id=1, source_target_pairs={{0,1},{1,2},{2,3},{3,4},{4,5},{5,6},{6,7},{8,9},{9,10},{10,11},{11... | collective-permute-start | bytes 2168 | tf_op jit(solution)/shard_map/ppermute | solution.py:15
  422.5 22.3 %collective-permute-start.41 = (f32[10,18,1]{2,1,0:T(8,128)S(1)}, f32[10,18,1]{2,1,0:T(8,128)S(1)}, u32[]{:S(2)}, u32[]{:S(2)}) collective-permute-start(f32[10,18,1]{2,1,0:T(8,128)S(1)} %get-tuple-element.113), channel_id=1, source_target_pairs={{1,0},{2,1},{3,2},{4,3},{5,4},{6,5},{7,6},{9,8},{10,9},{11,10},{12... | collective-permute-start | bytes 2168 | tf_op jit(solution)/shard_map/ppermute | solution.py:18
  488.3 16.6 %collective-permute-start.46 = (f32[10,18,1]{2,1,0:T(8,128)S(1)}, f32[10,18,1]{2,1,0:T(8,128)S(1)}, u32[]{:S(2)}, u32[]{:S(2)}) collective-permute-start(f32[10,18,1]{2,1,0:T(8,128)S(1)} %get-tuple-element.111), channel_id=1, source_target_pairs={{0,1},{1,2},{2,3},{3,4},{4,5},{5,6},{6,7},{8,9},{9,10},{10,11},{11... | collective-permute-start | bytes 2168 | tf_op jit(solution)/shard_map/ppermute | solution.py:15
  524.2 19.6 %collective-permute-start.53 = (f32[10,18,1]{2,1,0:T(8,128)S(1)}, f32[10,18,1]{2,1,0:T(8,128)S(1)}, u32[]{:S(2)}, u32[]{:S(2)}) collective-permute-start(f32[10,18,1]{2,1,0:T(8,128)S(1)} %get-tuple-element.110), channel_id=1, source_target_pairs={{1,0},{2,1},{3,2},{4,3},{5,4},{6,5},{7,6},{9,8},{10,9},{11,10},{12... | collective-permute-start | bytes 2168 | tf_op jit(solution)/shard_map/ppermute | solution.py:18
  528.7 16.3 %collective-permute-start.52 = (f32[10,18,1]{2,1,0:T(8,128)S(1)}, f32[10,18,1]{2,1,0:T(8,128)S(1)}, u32[]{:S(2)}, u32[]{:S(2)}) collective-permute-start(f32[10,18,1]{2,1,0:T(8,128)S(1)} %get-tuple-element.109), channel_id=1, source_target_pairs={{0,1},{1,2},{2,3},{3,4},{4,5},{5,6},{6,7},{8,9},{9,10},{10,11},{11... | collective-permute-start | bytes 2168 | tf_op jit(solution)/shard_map/ppermute | solution.py:15
  533.7 30.2 %collective-permute-start.4 = (f32[18,34,1]{2,1,0:T(8,128)S(1)}, f32[18,34,1]{2,1,0:T(8,128)S(1)}, u32[]{:S(2)}, u32[]{:S(2)}) collective-permute-start(f32[18,34,1]{2,1,0:T(8,128)S(1)} %get-tuple-element.74), channel_id=1, source_target_pairs={{0,1},{1,2},{2,3},{3,4},{4,5},{5,6},{6,7},{8,9},{9,10},{10,11},{11... | collective-permute-start | bytes 7352 | tf_op jit(solution)/shard_map/ppermute | solution.py:15
  535.6 28.3 %collective-permute-start.5 = (f32[18,34,1]{2,1,0:T(8,128)S(1)}, f32[18,34,1]{2,1,0:T(8,128)S(1)}, u32[]{:S(2)}, u32[]{:S(2)}) collective-permute-start(f32[18,34,1]{2,1,0:T(8,128)S(1)} %get-tuple-element.73), channel_id=1, source_target_pairs={{1,0},{2,1},{3,2},{4,3},{5,4},{6,5},{7,6},{9,8},{10,9},{11,10},{12... | collective-permute-start | bytes 7352 | tf_op jit(solution)/shard_map/ppermute | solution.py:18
  584.9 16.7 %collective-permute-start.57 = (f32[10,1,64]{2,1,0:T(1,128)S(1)}, f32[10,1,64]{2,1,0:T(1,128)S(1)}, u32[]{:S(2)}, u32[]{:S(2)}) collective-permute-start(f32[10,1,64]{2,1,0:T(1,128)S(1)} %get-tuple-element.120), channel_id=1, source_target_pairs={{8,0},{16,8},{24,16},{32,24},{40,32},{48,40},{56,48},{9,1},{17,9},... | collective-permute-start | bytes 7688 | tf_op jit(solution)/shard_map/ppermute | solution.py:18
  590.8 24.7 %collective-permute-start.11 = (f32[18,34,1]{2,1,0:T(8,128)S(1)}, f32[18,34,1]{2,1,0:T(8,128)S(1)}, u32[]{:S(2)}, u32[]{:S(2)}) collective-permute-start(f32[18,34,1]{2,1,0:T(8,128)S(1)} %get-tuple-element.72), channel_id=1, source_target_pairs={{1,0},{2,1},{3,2},{4,3},{5,4},{6,5},{7,6},{9,8},{10,9},{11,10},{12... | collective-permute-start | bytes 7352 | tf_op jit(solution)/shard_map/ppermute | solution.py:18
  599.7 24.9 %collective-permute-start.10 = (f32[18,34,1]{2,1,0:T(8,128)S(1)}, f32[18,34,1]{2,1,0:T(8,128)S(1)}, u32[]{:S(2)}, u32[]{:S(2)}) collective-permute-start(f32[18,34,1]{2,1,0:T(8,128)S(1)} %get-tuple-element.71), channel_id=1, source_target_pairs={{0,1},{1,2},{2,3},{3,4},{4,5},{5,6},{6,7},{8,9},{9,10},{10,11},{11... | collective-permute-start | bytes 7352 | tf_op jit(solution)/shard_map/ppermute | solution.py:15
  630.8 19.4 %collective-permute-start.59 = (f32[10,18,1]{2,1,0:T(8,128)S(1)}, f32[10,18,1]{2,1,0:T(8,128)S(1)}, u32[]{:S(2)}, u32[]{:S(2)}) collective-permute-start(f32[10,18,1]{2,1,0:T(8,128)S(1)} %get-tuple-element.108), channel_id=1, source_target_pairs={{1,0},{2,1},{3,2},{4,3},{5,4},{6,5},{7,6},{9,8},{10,9},{11,10},{12... | collective-permute-start | bytes 2168 | tf_op jit(solution)/shard_map/ppermute | solution.py:18
  652.8 15.1 %collective-permute-start.17 = (f32[18,34,1]{2,1,0:T(8,128)S(1)}, f32[18,34,1]{2,1,0:T(8,128)S(1)}, u32[]{:S(2)}, u32[]{:S(2)}) collective-permute-start(f32[18,34,1]{2,1,0:T(8,128)S(1)} %get-tuple-element.70), channel_id=1, source_target_pairs={{1,0},{2,1},{3,2},{4,3},{5,4},{6,5},{7,6},{9,8},{10,9},{11,10},{12... | collective-permute-start | bytes 7352 | tf_op jit(solution)/shard_map/ppermute | solution.py:18
  658.5 20.3 %collective-permute-start.16 = (f32[18,34,1]{2,1,0:T(8,128)S(1)}, f32[18,34,1]{2,1,0:T(8,128)S(1)}, u32[]{:S(2)}, u32[]{:S(2)}) collective-permute-start(f32[18,34,1]{2,1,0:T(8,128)S(1)} %get-tuple-element.69), channel_id=1, source_target_pairs={{0,1},{1,2},{2,3},{3,4},{4,5},{5,6},{6,7},{8,9},{9,10},{10,11},{11... | collective-permute-start | bytes 7352 | tf_op jit(solution)/shard_map/ppermute | solution.py:15
  662.0 23.1 %collective-permute-start.61 = (f32[1,16,64]{2,1,0:T(8,128)S(1)}, f32[1,16,64]{2,1,0:T(8,128)S(1)}, u32[]{:S(2)}, u32[]{:S(2)}) collective-permute-start(f32[1,16,64]{2,1,0:T(8,128)S(1)} %get-tuple-element.130), channel_id=1, source_target_pairs={{64,0},{128,64},{192,128},{65,1},{129,65},{193,129},{66,2},{130,66... | collective-permute-start | bytes 12296 | tf_op jit(solution)/shard_map/ppermute | solution.py:18
  666.6 18.5 %collective-permute-start.60 = (f32[1,16,64]{2,1,0:T(8,128)S(1)}, f32[1,16,64]{2,1,0:T(8,128)S(1)}, u32[]{:S(2)}, u32[]{:S(2)}) collective-permute-start(f32[1,16,64]{2,1,0:T(8,128)S(1)} %get-tuple-element.129), channel_id=1, source_target_pairs={{0,64},{64,128},{128,192},{1,65},{65,129},{129,193},{2,66},{66,130... | collective-permute-start | bytes 12296 | tf_op jit(solution)/shard_map/ppermute | solution.py:15
  679.3 28.6 %collective-permute-start.19 = (f32[1,32,128]{2,1,0:T(8,128)S(1)}, f32[1,32,128]{2,1,0:T(8,128)S(1)}, u32[]{:S(2)}, u32[]{:S(2)}) collective-permute-start(f32[1,32,128]{2,1,0:T(8,128)S(1)} %get-tuple-element.96), channel_id=1, source_target_pairs={{64,0},{128,64},{192,128},{65,1},{129,65},{193,129},{66,2},{130,66... | collective-permute-start | bytes 49160 | tf_op jit(solution)/shard_map/ppermute | solution.py:18
  683.8 24.1 %collective-permute-start.18 = (f32[1,32,128]{2,1,0:T(8,128)S(1)}, f32[1,32,128]{2,1,0:T(8,128)S(1)}, u32[]{:S(2)}, u32[]{:S(2)}) collective-permute-start(f32[1,32,128]{2,1,0:T(8,128)S(1)} %get-tuple-element.95), channel_id=1, source_target_pairs={{0,64},{64,128},{128,192},{1,65},{65,129},{129,193},{2,66},{66,130... | collective-permute-start | bytes 49160 | tf_op jit(solution)/shard_map/ppermute | solution.py:15
  685.1 28.4 %collective-permute-start.63 = (f32[10,1,64]{2,1,0:T(1,128)S(1)}, f32[10,1,64]{2,1,0:T(1,128)S(1)}, u32[]{:S(2)}, u32[]{:S(2)}) collective-permute-start(f32[10,1,64]{2,1,0:T(1,128)S(1)} %get-tuple-element.118), channel_id=1, source_target_pairs={{8,0},{16,8},{24,16},{32,24},{40,32},{48,40},{56,48},{9,1},{17,9},... | collective-permute-start | bytes 7688 | tf_op jit(solution)/shard_map/ppermute | solution.py:18
  687.1 26.5 %collective-permute-start.62 = (f32[10,1,64]{2,1,0:T(1,128)S(1)}, f32[10,1,64]{2,1,0:T(1,128)S(1)}, u32[]{:S(2)}, u32[]{:S(2)}) collective-permute-start(f32[10,1,64]{2,1,0:T(1,128)S(1)} %get-tuple-element.117), channel_id=1, source_target_pairs={{0,8},{8,16},{16,24},{24,32},{32,40},{40,48},{48,56},{1,9},{9,17},... | collective-permute-start | bytes 7688 | tf_op jit(solution)/shard_map/ppermute | solution.py:15
  714.5 19.2 %collective-permute-start.23 = (f32[18,34,1]{2,1,0:T(8,128)S(1)}, f32[18,34,1]{2,1,0:T(8,128)S(1)}, u32[]{:S(2)}, u32[]{:S(2)}) collective-permute-start(f32[18,34,1]{2,1,0:T(8,128)S(1)} %get-tuple-element.68), channel_id=1, source_target_pairs={{1,0},{2,1},{3,2},{4,3},{5,4},{6,5},{7,6},{9,8},{10,9},{11,10},{12... | collective-permute-start | bytes 7352 | tf_op jit(solution)/shard_map/ppermute | solution.py:18
  720.7 26.5 %collective-permute-start.22 = (f32[18,34,1]{2,1,0:T(8,128)S(1)}, f32[18,34,1]{2,1,0:T(8,128)S(1)}, u32[]{:S(2)}, u32[]{:S(2)}) collective-permute-start(f32[18,34,1]{2,1,0:T(8,128)S(1)} %get-tuple-element.67), channel_id=1, source_target_pairs={{0,1},{1,2},{2,3},{3,4},{4,5},{5,6},{6,7},{8,9},{9,10},{10,11},{11... | collective-permute-start | bytes 7352 | tf_op jit(solution)/shard_map/ppermute | solution.py:15
  723.8 29.2 %collective-permute-start.65 = (f32[10,18,1]{2,1,0:T(8,128)S(1)}, f32[10,18,1]{2,1,0:T(8,128)S(1)}, u32[]{:S(2)}, u32[]{:S(2)}) collective-permute-start(f32[10,18,1]{2,1,0:T(8,128)S(1)} %get-tuple-element.106), channel_id=1, source_target_pairs={{1,0},{2,1},{3,2},{4,3},{5,4},{6,5},{7,6},{9,8},{10,9},{11,10},{12... | collective-permute-start | bytes 2168 | tf_op jit(solution)/shard_map/ppermute | solution.py:18
  730.9 22.1 %collective-permute-start.64 = (f32[10,18,1]{2,1,0:T(8,128)S(1)}, f32[10,18,1]{2,1,0:T(8,128)S(1)}, u32[]{:S(2)}, u32[]{:S(2)}) collective-permute-start(f32[10,18,1]{2,1,0:T(8,128)S(1)} %get-tuple-element.105), channel_id=1, source_target_pairs={{0,1},{1,2},{2,3},{3,4},{4,5},{5,6},{6,7},{8,9},{9,10},{10,11},{11... | collective-permute-start | bytes 2168 | tf_op jit(solution)/shard_map/ppermute | solution.py:15
  756.2 18.7 %collective-permute-start.27 = (f32[18,1,128]{2,1,0:T(1,128)S(1)}, f32[18,1,128]{2,1,0:T(1,128)S(1)}, u32[]{:S(2)}, u32[]{:S(2)}) collective-permute-start(f32[18,1,128]{2,1,0:T(1,128)S(1)} %get-tuple-element.80), channel_id=1, source_target_pairs={{8,0},{16,8},{24,16},{32,24},{40,32},{48,40},{56,48},{9,1},{17,9},... | collective-permute-start | bytes 27656 | tf_op jit(solution)/shard_map/ppermute | solution.py:18
  759.8 15.1 %collective-permute-start.26 = (f32[18,1,128]{2,1,0:T(1,128)S(1)}, f32[18,1,128]{2,1,0:T(1,128)S(1)}, u32[]{:S(2)}, u32[]{:S(2)}) collective-permute-start(f32[18,1,128]{2,1,0:T(1,128)S(1)} %get-tuple-element.79), channel_id=1, source_target_pairs={{0,8},{8,16},{16,24},{24,32},{32,40},{40,48},{48,56},{1,9},{9,17},... | collective-permute-start | bytes 27656 | tf_op jit(solution)/shard_map/ppermute | solution.py:15
  775.2 16.3 %collective-permute-start.29 = (f32[18,34,1]{2,1,0:T(8,128)S(1)}, f32[18,34,1]{2,1,0:T(8,128)S(1)}, u32[]{:S(2)}, u32[]{:S(2)}) collective-permute-start(f32[18,34,1]{2,1,0:T(8,128)S(1)} %get-tuple-element.66), channel_id=1, source_target_pairs={{1,0},{2,1},{3,2},{4,3},{5,4},{6,5},{7,6},{9,8},{10,9},{11,10},{12... | collective-permute-start | bytes 7352 | tf_op jit(solution)/shard_map/ppermute | solution.py:18
  777.6 32.1 %collective-permute-start.28 = (f32[18,34,1]{2,1,0:T(8,128)S(1)}, f32[18,34,1]{2,1,0:T(8,128)S(1)}, u32[]{:S(2)}, u32[]{:S(2)}) collective-permute-start(f32[18,34,1]{2,1,0:T(8,128)S(1)} %get-tuple-element.65), channel_id=1, source_target_pairs={{0,1},{1,2},{2,3},{3,4},{4,5},{5,6},{6,7},{8,9},{9,10},{10,11},{11... | collective-permute-start | bytes 7352 | tf_op jit(solution)/shard_map/ppermute | solution.py:15
  784.4 32.0 %collective-permute-start.69 = (f32[10,1,64]{2,1,0:T(1,128)S(1)}, f32[10,1,64]{2,1,0:T(1,128)S(1)}, u32[]{:S(2)}, u32[]{:S(2)}) collective-permute-start(f32[10,1,64]{2,1,0:T(1,128)S(1)} %get-tuple-element.116), channel_id=1, source_target_pairs={{8,0},{16,8},{24,16},{32,24},{40,32},{48,40},{56,48},{9,1},{17,9},... | collective-permute-start | bytes 7688 | tf_op jit(solution)/shard_map/ppermute | solution.py:18
  786.4 30.0 %collective-permute-start.68 = (f32[10,1,64]{2,1,0:T(1,128)S(1)}, f32[10,1,64]{2,1,0:T(1,128)S(1)}, u32[]{:S(2)}, u32[]{:S(2)}) collective-permute-start(f32[10,1,64]{2,1,0:T(1,128)S(1)} %get-tuple-element.115), channel_id=1, source_target_pairs={{0,8},{8,16},{16,24},{24,32},{32,40},{40,48},{48,56},{1,9},{9,17},... | collective-permute-start | bytes 7688 | tf_op jit(solution)/shard_map/ppermute | solution.py:15
  819.6 15.0 %collective-permute-start.33 = (f32[18,1,128]{2,1,0:T(1,128)S(1)}, f32[18,1,128]{2,1,0:T(1,128)S(1)}, u32[]{:S(2)}, u32[]{:S(2)}) collective-permute-start(f32[18,1,128]{2,1,0:T(1,128)S(1)} %get-tuple-element.78), channel_id=1, source_target_pairs={{8,0},{16,8},{24,16},{32,24},{40,32},{48,40},{56,48},{9,1},{17,9},... | collective-permute-start | bytes 27656 | tf_op jit(solution)/shard_map/ppermute | solution.py:18
  825.3 20.2 %collective-permute-start.71 = (f32[10,18,1]{2,1,0:T(8,128)S(1)}, f32[10,18,1]{2,1,0:T(8,128)S(1)}, u32[]{:S(2)}, u32[]{:S(2)}) collective-permute-start(f32[10,18,1]{2,1,0:T(8,128)S(1)} %get-tuple-element.104), channel_id=1, source_target_pairs={{1,0},{2,1},{3,2},{4,3},{5,4},{6,5},{7,6},{9,8},{10,9},{11,10},{12... | collective-permute-start | bytes 2168 | tf_op jit(solution)/shard_map/ppermute | solution.py:18
  827.3 18.3 %collective-permute-start.70 = (f32[10,18,1]{2,1,0:T(8,128)S(1)}, f32[10,18,1]{2,1,0:T(8,128)S(1)}, u32[]{:S(2)}, u32[]{:S(2)}) collective-permute-start(f32[10,18,1]{2,1,0:T(8,128)S(1)} %get-tuple-element.103), channel_id=1, source_target_pairs={{0,1},{1,2},{2,3},{3,4},{4,5},{5,6},{6,7},{8,9},{9,10},{10,11},{11... | collective-permute-start | bytes 2168 | tf_op jit(solution)/shard_map/ppermute | solution.py:15
  835.6 15.8 %collective-permute-start.35 = (f32[18,34,1]{2,1,0:T(8,128)}, f32[18,34,1]{2,1,0:T(8,128)}, u32[]{:S(2)}, u32[]{:S(2)}) collective-permute-start(f32[18,34,1]{2,1,0:T(8,128)} %get-tuple-element.64), channel_id=1, source_target_pairs={{1,0},{2,1},{3,2},{4,3},{5,4},{6,5},{7,6},{9,8},{10,9},{11,10},{12... | collective-permute-start | bytes 7352 | tf_op jit(solution)/shard_map/ppermute | solution.py:18
  838.4 24.4 %collective-permute-start.34 = (f32[18,34,1]{2,1,0:T(8,128)}, f32[18,34,1]{2,1,0:T(8,128)}, u32[]{:S(2)}, u32[]{:S(2)}) collective-permute-start(f32[18,34,1]{2,1,0:T(8,128)} %get-tuple-element.63), channel_id=1, source_target_pairs={{0,1},{1,2},{2,3},{3,4},{4,5},{5,6},{6,7},{8,9},{9,10},{10,11},{11... | collective-permute-start | bytes 7352 | tf_op jit(solution)/shard_map/ppermute | solution.py:15
  871.5 15.3 %collective-permute-start.165 = (f32[18,1,128]{2,1,0:T(1,128)S(1)}, f32[18,1,128]{2,1,0:T(1,128)S(1)}, u32[]{:S(2)}, u32[]{:S(2)}) collective-permute-start(f32[18,1,128]{2,1,0:T(1,128)S(1)} %get-tuple-element.76), channel_id=1, source_target_pairs={{8,0},{16,8},{24,16},{32,24},{40,32},{48,40},{56,48},{9,1},{17,9},... | collective-permute-start | bytes 27656 | tf_op jit(solution)/shard_map/ppermute | solution.py:18
  887.9 16.3 %collective-permute-start.167 = (f32[18,34,1]{2,1,0:T(8,128)S(1)}, f32[18,34,1]{2,1,0:T(8,128)S(1)}, u32[]{:S(2)}, u32[]{:S(2)}) collective-permute-start(f32[18,34,1]{2,1,0:T(8,128)S(1)} %get-tuple-element.62), channel_id=1, source_target_pairs={{1,0},{2,1},{3,2},{4,3},{5,4},{6,5},{7,6},{9,8},{10,9},{11,10},{12... | collective-permute-start | bytes 7352 | tf_op jit(solution)/shard_map/ppermute | solution.py:18
  889.8 32.5 %collective-permute-start.166 = (f32[18,34,1]{2,1,0:T(8,128)S(1)}, f32[18,34,1]{2,1,0:T(8,128)S(1)}, u32[]{:S(2)}, u32[]{:S(2)}) collective-permute-start(f32[18,34,1]{2,1,0:T(8,128)S(1)} %get-tuple-element.61), channel_id=1, source_target_pairs={{0,1},{1,2},{2,3},{3,4},{4,5},{5,6},{6,7},{8,9},{9,10},{10,11},{11... | collective-permute-start | bytes 7352 | tf_op jit(solution)/shard_map/ppermute | solution.py:15
  (124 other events, 1092.8 us)
where the time goes:
time: 928 us; the launch traced here: 923 us
  starting transfers between devices  616 us (66%)
  waiting for transfers between devices  232 us (25%)
  local copies, waits for them, and re-layouts  47.3 us (5%)
  other arithmetic  24.1 us (3%)
    ppermute x84, starting transfers between devices, padded_2(): lax.ppermute(lax.slice_in_dim(block, 0, width, axis=dim), axis, backward)  325 us
    ppermute x84, starting transfers between devices, padded_2(): lax.ppermute(lax.slice_in_dim(block, block.shape[dim] - width, None, axis...  291 us
    ppermute x84, waiting for transfers between devices, padded_2(): lax.ppermute(lax.slice_in_dim(block, block.shape[dim] - width, None, axis...  172 us
    ppermute x84, waiting for transfers between devices, padded_2(): lax.ppermute(lax.slice_in_dim(block, 0, width, axis=dim), axis, backward)  60 us
    reshape x4, local copies, waits for them, and re-layouts, restrict_sum(): field.reshape(size_x // 2, 2, size_y // 2, 2, size_z // 2, 2)  39.3 us
  transfers between devices with their start and end apart: 168, of which 49 were waited for; matrix products, arithmetic and copies ran while one was open for 4% of the time, Pallas kernels for 0%

commit v1 on v0

v1 whole, which is shorter than its diff:
```python
import jax
import jax.numpy as jnp
from jax import lax
from jax.experimental import pallas as pl
from jax.experimental.pallas import tpu as pltpu
from jax.sharding import PartitionSpec as P

f32 = jnp.float32
MESH = pl.DeviceIdType.MESH

CENTRE = (2.0 + 0.3) / 2.0
HALF = (2.0 - 0.3) / 2.0
SHARP = CENTRE / HALF
W0 = 1.0 / SHARP
W1 = 1.0 / (2.0 * SHARP - W0)
W2 = 1.0 / (2.0 * SHARP - W1)
W3 = 1.0 / (2.0 * SHARP - W2)
B0 = 1.0 / CENTRE
A1, B1 = W1 * W0, 2.0 * W1 / HALF
A2, B2 = W2 * W1, 2.0 * W2 / HALF
A3, B3 = W3 * W2, 2.0 * W3 / HALF

NEAR = [(dx, dy) for dx in (-1, 0, 1) for dy in (-1, 0, 1) if (dx, dy) != (0, 0)]
PLANE = [(a, b) for a in range(4) for b in range(8) if (a, b) != (0, 0)]


def lanes(rows):
    return lax.broadcasted_iota(jnp.int32, (rows, 128), 1)


def rowid(rows):
    return lax.broadcasted_iota(jnp.int32, (rows, 128), 0)


def gat(x, idx):
    return jnp.take_along_axis(x, idx, axis=1, mode="promise_in_bounds")


def roll(x, shift):
    return pltpu.roll(x, shift, 1)


def loop(lo, hi, body):
    def step(i, c):
        body(i)
        return c

    lax.fori_loop(lo, hi, step, 0)


def rem(a, n):
    return lax.rem(a, n)


class Level:
    def __init__(self, refs, planes, rows, factor, mask):
        self.K, self.R, self.CX, self.CY, self.CZ, self.ID, self.VA, self.VB = refs
        self.X, self.Y, self.h, self.mask = planes, rows, 0.5 * factor, mask

    def clear(self):
        Y = self.Y
        pad = jnp.zeros((8, 128), f32)

        def body(i):
            for ref in (self.K, self.VA, self.VB):
                ref[i, 0:8] = pad
                ref[i, 8 + Y : 16 + Y] = pad

        loop(0, self.X, body)
        full = jnp.zeros((Y, 128), f32)
        for i in (0, self.X - 1):
            for ref in (self.VA, self.VB, self.K):
                ref[i, 8 : 8 + Y] = full

    def build(self):
        Y, h, K = self.Y, self.h, self.K

        def body(i):
            k = K[i, 8 : 8 + Y]
            low = h * (k + K[i - 1, 8 : 8 + Y])
            high = h * (k + K[i + 1, 8 : 8 + Y])
            self.CX[i] = low
            self.CX[i + 1] = high
            self.CY[i] = h * (K[i, 8 : 16 + Y] + K[i, 7 : 15 + Y])
            cz = h * (k + roll(k, 1))
            self.CZ[i] = cz
            ylow = h * (k + K[i, 7 : 7 + Y])
            yhigh = h * (k + K[i, 9 : 9 + Y])
            d = low + high + ylow + yhigh + cz + roll(cz, 127)
            inv = jnp.where(self.mask(i), 1.0 / d, 0.0)
            self.ID[i] = inv
            self.VA[i, 8 : 8 + Y] = B0 * (self.R[i] * inv)

        loop(1, self.X - 1, body)

    def flux(self, V, i):
        Y = self.Y
        v = V[i, 8 : 8 + Y]
        out = self.CX[i] * (v - V[i - 1, 8 : 8 + Y])
        out = out + self.CX[i + 1] * (v - V[i + 1, 8 : 8 + Y])
        out = out + self.CY[i, 0:Y] * (v - V[i, 7 : 7 + Y])
        out = out + self.CY[i, 1 : 1 + Y] * (v - V[i, 9 : 9 + Y])
        fz = self.CZ[i] * (v - roll(v, 1))
        return v, out + (fz - roll(fz, 127))

    def step(self, src, dst, a, b, shrink, first=False):
        Y = self.Y

        def body(i):
            v, av = self.flux(src, i)
            new = v + b * (self.ID[i] * (self.R[i] - av))
            if first:
                new = new + a * v
            elif a != 0.0:
                new = new + a * (v - dst[i, 8 : 8 + Y])
            dst[i, 8 : 8 + Y] = new

        loop(1 + shrink, self.X - 1 - shrink, body)

    def smooth6(self, after=None, trim=True):
        plan = [
            (self.VA, self.VB, A1, B1, True),
            (self.VB, self.VA, A2, B2, False),
            (self.VA, self.VB, 0.0, B0, False),
            (self.VB, self.VA, A1, B1, False),
            (self.VA, self.VB, A2, B2, False),
        ]
        for n, (src, dst, a, b, first) in enumerate(plan):
            self.step(src, dst, a, b, n + 1 if trim else 0, first)
            if after is not None and n < 4:
                after(dst)


def kernel(r_in, k_in, corr_out, res_out, *s):
    (E0, E1, E23, XB, PB, RK2, T, TH, RES, HV, KH, sem_loc, e0s, e0r, e1s, e1r, gs, gr, bs, br, xs, xr, cs, cr, *lv) = s
    gx, gy, gz = lax.axis_index("gx"), lax.axis_index("gy"), lax.axis_index("gz")
    own = gx * 8 + gy

    bar = pltpu.get_barrier_semaphore()

    def peer(a, b):
        return rem(gx + a, 4), rem(gy + b, 8)

    for a, b in PLANE:
        px, py = peer(a, b)
        pl.semaphore_signal(bar, inc=1, device_id={"gx": px, "gy": py}, device_id_type=MESH)

    @pl.when(gz > 0)
    def _():
        pl.semaphore_signal(bar, inc=1, device_id={"gz": gz - 1}, device_id_type=MESH)

    @pl.when(gz < 7)
    def _():
        pl.semaphore_signal(bar, inc=1, device_id={"gz": gz + 1}, device_id_type=MESH)

    def yz(rows, ylo, ny, zlo, zown, zhi):
        y = rowid(rows) + ylo
        l = lanes(rows)
        low = jnp.where(gz > 0, 128 - zlo, 128)
        high = jnp.where(gz < 7, zown + zhi, zown)
        return (y >= 0) & (y < ny) & ((l < high) | (l >= low))

    def with_x(base, rows, x, nx):
        xv = jnp.zeros((rows, 128), jnp.int32) + x
        return base & (xv >= 0) & (xv < nx)

    def mask0(i):
        return with_x(yz(48, 32 * gy - 8, 256, 0, 128, 0), 48, 16 * gx + i - 7, 64)

    def group(rows):
        l = lanes(rows)
        g = jnp.where(l >= 84, 2, jnp.where(l >= 42, 1, 0))
        return l, g, l - 42 * g

    def masks(i):
        l, g, zz = group(48)
        y = rowid(48) + (32 * gy - 8)
        x = 10 * g + (16 * gx + i - 8)
        low = jnp.where(gz > 0, 0, 8)
        high = jnp.where(gz < 7, 42, 34)
        return (y >= 0) & (y < 256) & (x >= 0) & (x < 64) & (zz >= low) & (zz < high) & (l < 126)

    def mask1(i):
        return with_x(yz(32, 16 * gy - 8, 128, 8, 64, 8), 32, 8 * gx + i - 7, 32)

    def mask2(i):
        return with_x(yz(24, 8 * gy - 8, 64, 8, 32, 8), 24, 4 * gx + i - 7, 16)

    def mask3(i):
        return yz(32, 0, 32, 16, 16, 16)

    def mask4(i):
        return yz(16, 0, 16, 8, 8, 8)

    L0 = Level(lv[0:8], 30, 48, 1.0, mask0)
    LS = Level(lv[8:16], 12, 48, 1.0, masks)
    L1 = Level(lv[16:24], 22, 32, 2.0, mask1)
    L2 = Level(lv[24:32], 18, 24, 4.0, mask2)
    L3 = Level(lv[32:40], 10, 32, 8.0, mask3)
    L4 = Level(lv[40:48], 6, 16, 16.0, mask4)

    loc = [
        pltpu.make_async_copy(ref, E0.at[n, 7:23, 8:40], sem_loc.at[n]) for n, ref in enumerate((r_in, k_in))
    ]
    for c in loc:
        c.start()

    l32 = lanes(32)
    zero32 = jnp.zeros((32, 128), f32)

    def pack0(x, c):
        r8, k8 = roll(r_in[x], 8 * x), roll(k_in[x], 8 * x)
        here, before = (l32 >> 3) == x, (l32 >> 3) == ((x + 15) & 15)
        return (
            jnp.where(here, r8, c[0]),
            jnp.where(here, k8, c[1]),
            jnp.where(before, r8, c[2]),
            jnp.where(before, k8, c[3]),
        )

    packed = lax.fori_loop(0, 16, pack0, (zero32,) * 4)
    PB[0, 0], PB[0, 1] = packed[0], packed[1]
    PB[1, 0], PB[1, 1] = roll(packed[2], 8), roll(packed[3], 8)

    def pair(x, rows):
        l = lanes(rows)
        return gat(x, (2 * l) & 127) + gat(x, (2 * l + 1) & 127)

    l16 = lanes(16)

    def down1(x, c):
        out = []
        for ref in (r_in, k_in):
            t = (ref[2 * x, pl.ds(0, 16, stride=2)] + ref[2 * x, pl.ds(1, 16, stride=2)]) + (
                ref[2 * x + 1, pl.ds(0, 16, stride=2)] + ref[2 * x + 1, pl.ds(1, 16, stride=2)]
            )
            out.append(pair(t, 16))
        rk = jnp.where(l16 < 64, out[0], 0.125 * out[1])
        E1[7 + x, 8:24] = rk
        here = ((l16 & 63) >> 3) == x
        return (
            jnp.where(here, roll(rk, 8 * x), c[0]),
            jnp.where(here, roll(rk, (8 * x + 72) & 127), c[1]),
        )

    zero16 = jnp.zeros((16, 128), f32)
    low1, high1 = lax.fori_loop(0, 8, down1, (zero16, zero16))
    for side, val in enumerate((low1, high1)):
        PB[side, 2, 0:8] = val[0:8]
        PB[side, 2, 24:32] = val[8:16]

    l8 = lanes(8)
    zero8 = jnp.zeros((8, 128), f32)

    def down2(x, c):
        def part(p, n):
            return E1[7 + 2 * x + p, pl.ds(8 + n, 8, stride=2)]

        t = (part(0, 0) + part(0, 1)) + (part(1, 0) + part(1, 1))
        rk = pair(t, 8)
        rk = jnp.where(((l8 >> 5) & 1) == 1, 0.125 * rk, rk)
        RK2[x] = rk
        here, edge = (l8 >> 5) == x, (l8 < 64) & (((l8 & 31) >> 3) == x)
        return (
            jnp.where(here, roll(rk, 32 * x), c[0]),
            jnp.where(here, roll(rk, (32 * x + 96) & 127), c[1]),
            jnp.where(edge, roll(rk, 8 * x), c[2]),
            jnp.where(edge, roll(rk, (8 * x + 104) & 127), c[3]),
        )

    r2, k2, low2, high2 = lax.fori_loop(0, 4, down2, (zero8,) * 4)
    l4 = lanes(4)
    rk3 = []
    for x in range(2):
        t = (RK2[2 * x, pl.ds(0, 4, stride=2)] + RK2[2 * x, pl.ds(1, 4, stride=2)]) + (
            RK2[2 * x + 1, pl.ds(0, 4, stride=2)] + RK2[2 * x + 1, pl.ds(1, 4, stride=2)]
        )
        T[0:4], T[4:8] = t, t
        t = pair(T[0:8], 8)
        rk3.append(jnp.where(((l8 >> 4) & 1) == 1, 0.125 * t, t))
    m3 = jnp.where(((l8 >> 5) & 1) == 0, rk3[0], rk3[1])
    E23[own, 0], E23[own, 1], E23[own, 2] = r2, k2, m3
    RK2[0] = jnp.where(l8 < 64, low2, m3)
    RK2[1] = jnp.where(l8 < 64, high2, m3)

    for L in (L0, LS, L1, L2, L3, L4):
        L.clear()

    pl.semaphore_wait(bar, 31 + jnp.where(gz > 0, 1, 0) + jnp.where(gz < 7, 1, 0))

    def zcopies(side):
        dev = {"gz": gz - 1 if side == 0 else gz + 1}
        land = 1 - side
        pieces = [
            (PB.at[side, 0:2], XB.at[1, land, 0:2, 8:40]),
            (PB.at[side, 2, 0:8], XB.at[1, land, 2, 8:16]),
            (PB.at[side, 2, 24:32], XB.at[1, land, 2, 32:40]),
            (RK2.at[side], E23.at[own, 3 + land]),
        ]
        return [
            pltpu.make_async_remote_copy(
                src_ref=src, dst_ref=dst, send_sem=bs.at[side, n], recv_sem=br.at[side, n],
                device_id=dev, device_id_type=MESH,
            )
            for n, (src, dst) in enumerate(pieces)
        ]

    def each(cond, copies, what):
        @pl.when(cond)
        def _():
            for c in copies:
                getattr(c, what)()

    zdown, zup = zcopies(0), zcopies(1)
    each(gz > 0, zdown[::-1], "start")
    each(gz < 7, zup[::-1], "start")

    for c in loc:
        c.wait()

    def inside(dx, dy):
        return (gx + dx >= 0) & (gx + dx < 4) & (gy + dy >= 0) & (gy + dy < 8)

    SRC0X, DST0X = {-1: (7, 14), 0: (7, 23), 1: (16, 23)}, {-1: (23, 30), 0: (7, 23), 1: (0, 7)}
    SRC0Y, DST0Y = {-1: (8, 16), 0: (8, 40), 1: (32, 40)}, {-1: (40, 48), 0: (8, 40), 1: (0, 8)}
    SRC1X, DST1X = {-1: (7, 14), 0: (7, 15), 1: (8, 15)}, {-1: (15, 22), 0: (7, 15), 1: (0, 7)}
    SRC1Y, DST1Y = {-1: (8, 16), 0: (8, 24), 1: (16, 24)}, {-1: (24, 32), 0: (8, 24), 1: (0, 8)}

    def sl(pairs):
        return pl.ds(pairs[0], pairs[1] - pairs[0])

    def near_copies(make):
        return [(inside(dx, dy), inside(-dx, -dy), make(n, dx, dy)) for n, (dx, dy) in enumerate(NEAR)]

    def rc(src, dst, ss, rs, dev):
        return pltpu.make_async_remote_copy(
            src_ref=src, dst_ref=dst, send_sem=ss, recv_sem=rs, device_id=dev, device_id_type=MESH
        )

    def dev_near(dx, dy):
        return {"gx": gx + dx, "gy": gy + dy}

    c0 = near_copies(lambda n, dx, dy: rc(
        E0.at[:, sl(SRC0X[dx]), sl(SRC0Y[dy])], E0.at[:, sl(DST0X[dx]), sl(DST0Y[dy])], e0s.at[n], e0r.at[n], dev_near(dx, dy)))
    c1 = near_copies(lambda n, dx, dy: rc(
        E1.at[sl(SRC1X[dx]), sl(SRC1Y[dy])], E1.at[sl(DST1X[dx]), sl(DST1Y[dy])], e1s.at[n], e1r.at[n], dev_near(dx, dy)))
    cx = near_copies(lambda n, dx, dy: rc(
        XB.at[1, :, :, sl(SRC0Y[dy])], XB.at[1 - dx, :, :, sl(DST0Y[dy])], xs.at[n], xr.at[n], dev_near(dx, dy)))

    def close(a, b, sign):
        px, py = rem(gx + sign * a + 4, 4), rem(gy + sign * b + 8, 8)
        return (jnp.abs(px - gx) <= 2) & (jnp.abs(py - gy) <= 1)

    gather, gather_z = [], []
    for n, (a, b) in enumerate(PLANE):
        px, py = peer(a, b)
        dev = {"gx": px, "gy": py}
        wide = rc(E23.at[own, 0:3], E23.at[own, 0:3], gs.at[n], gr.at[n], dev)
        thin = rc(E23.at[own, 2:3], E23.at[own, 2:3], gs.at[n], gr.at[n], dev)
        gather.append((wide, thin, close(a, b, 1), close(a, b, -1)))
        gather_z.append(rc(E23.at[own, 3:5], E23.at[own, 3:5], cs.at[n], cr.at[n], dev))

    for ok, _, c in c0:
        each(ok, [c], "start")
    for ok, _, c in c1:
        each(ok, [c], "start")
    for wide, thin, near, _ in gather:
        each(near, [wide], "start")
        each(jnp.logical_not(near), [thin], "start")

    @pl.when(gz == 0)
    def _():
        for n in range(3):
            XB[1, 0, n, 8:40] = zero32
        E23[own, 3] = zero8

    @pl.when(gz == 7)
    def _():
        for n in range(3):
            XB[1, 1, n, 8:40] = zero32
        E23[own, 4] = zero8

    each(gz < 7, [zdown[3]], "wait_recv")
    each(gz > 0, [zup[3]], "wait_recv")
    for c in gather_z:
        c.start()
    each(gz < 7, zdown[0:3], "wait_recv")
    each(gz > 0, zup[0:3], "wait_recv")
    for ok, _, c in cx:
        each(ok, [c], "start")

    for _, okr, c in c0:
        each(okr, [c], "wait_recv")

    def load0(i):
        m = mask0(i)
        L0.K[i, 8:56] = jnp.where(m, E0[1, i], 0.0)
        L0.R[i] = jnp.where(m, E0[0, i], 0.0)

    loop(0, 30, load0)
    L0.build()
    L0.smooth6()

    for wide, thin, _, near in gather:
        each(near, [wide], "wait_recv")
        each(jnp.logical_not(near), [thin], "wait_recv")
    for c in gather_z:
        c.wait_recv()
    top = rowid(8) < 4
    in3 = yz(8, 0, 8, 16, 16, 16)
    for sx in range(4):
        def load3(q, sx=sx):
            sa, sb = sx * 8 + 2 * q, sx * 8 + 2 * q + 1
            m = jnp.where(top, E23[sa, 2], E23[sb, 2])
            lo = jnp.where(top, E23[sa, 3], E23[sb, 3])
            hi = jnp.where(top, E23[sa, 4], E23[sb, 4])
            row = pl.multiple_of(8 * q, 8)
            for xl in range(2):
                for isk in range(2):
                    at = 32 * xl + 16 * isk
                    out = jnp.where(
                        l8 < 16, roll(m, (128 - at) % 128),
                        jnp.where(l8 < 32, roll(hi, (16 - 64 - at) % 128), roll(lo, (112 - 64 - at) % 128)),
                    )
                    out = jnp.where(in3, out, 0.0)
                    if isk:
                        L3.K[1 + 2 * sx + xl, pl.ds(8 + row, 8)] = out
                    else:
                        L3.R[1 + 2 * sx + xl, pl.ds(row, 8)] = out

        loop(0, 4, load3)
    L3.build()
    L3.step(L3.VA, L3.VB, A1, B1, 0, True)

    def residue(i):
        _, av = L3.flux(L3.VB, i)
        RES[i - 1] = L3.R[i] - av

    loop(1, 9, residue)
    in4 = mask4(0)

    def down4(x):
        t = (RES[2 * x, pl.ds(0, 16, stride=2)] + RES[2 * x, pl.ds(1, 16, stride=2)]) + (
            RES[2 * x + 1, pl.ds(0, 16, stride=2)] + RES[2 * x + 1, pl.ds(1, 16, stride=2)]
        )
        L4.R[1 + x] = jnp.where(in4, pair(t, 16), 0.0)
        t = (L3.K[1 + 2 * x, pl.ds(8, 16, stride=2)] + L3.K[1 + 2 * x, pl.ds(9, 16, stride=2)]) + (
            L3.K[2 + 2 * x, pl.ds(8, 16, stride=2)] + L3.K[2 + 2 * x, pl.ds(9, 16, stride=2)]
        )
        L4.K[1 + x, 8:24] = jnp.where(in4, 0.125 * pair(t, 16), 0.0)

    loop(0, 4, down4)
    L4.build()
    L4.step(L4.VA, L4.VB, A1, B1, 0, True)
    L4.step(L4.VB, L4.VA, A2, B2, 0)
    L4.step(L4.VA, L4.VB, A3, B3, 0)

    def repeat_lanes(x, rows):
        l = lanes(rows)
        return gat(x, jnp.where(l < 96, l >> 1, (l >> 1) + 64))

    def repeat_rows(ref, x, rows):
        ref[pl.ds(0, rows, stride=2)] = x
        ref[pl.ds(1, rows, stride=2)] = x

    def up4(x):
        repeat_rows(T, repeat_lanes(L4.VB[1 + x, 8:24], 16), 16)
        for p in range(2):
            L3.VB[1 + 2 * x + p, 8:40] = L3.VB[1 + 2 * x + p, 8:40] + T[0:32]

    loop(0, 4, up4)
    L3.step(L3.VB, L3.VA, 0.0, B0, 0)
    L3.step(L3.VA, L3.VB, A1, B1, 0)

    def load2(i):
        xg = 4 * gx + i - 7 + 8
        sx = (xg >> 2) - 2
        xl = xg & 3
        scx = jnp.clip(sx, 0, 3)
        m = mask2(i)
        for n in range(3):
            sy = jnp.clip(gy + n - 1, 0, 7)
            slot = scx * 8 + sy
            r, k, lo, hi = E23[slot, 0], E23[slot, 1], E23[slot, 3], E23[slot, 4]
            mn = m[8 * n : 8 * n + 8]
            for isk, mid in ((0, r), (1, k)):
                at = 8 * xl + 32 * isk
                out = jnp.where(
                    l8 < 32, roll(mid, (128 - 32 * xl) & 127),
                    jnp.where(l8 < 64, roll(hi, (160 - at) & 127), roll(lo, (248 - at) & 127)),
                )
                out = jnp.where(mn, out, 0.0)
                if isk:
                    L2.K[i, 8 + 8 * n : 16 + 8 * n] = out
                else:
                    L2.R[i, 8 * n : 8 * n + 8] = out

    loop(0, 18, load2)
    L2.build()
    L2.smooth6()

    def up3(q):
        w = L3.VB[2 * gx + q, pl.ds(4 * gy + 4, 16)]
        repeat_rows(T, repeat_lanes(w, 16), 16)
        for p in range(2):
            L2.VB[2 * q + 5 + p, 8:32] = L2.VB[2 * q + 5 + p, 8:32] + T[0:24]

    loop(0, 4, up3)

    for _, okr, c in c1:
        each(okr, [c], "wait_recv")
    for _, okr, c in cx:
        each(okr, [c], "wait_recv")

    l32b = lanes(32)

    def load1(i):
        x = i - 7
        dx = jnp.where(x >= 0, 1, 0) + jnp.where(x >= 8, 1, 0)
        xl = x & 7
        m = mask1(i)
        main = E1[i]
        lo = jnp.concatenate([XB[dx, 0, 2, 0:16], XB[dx, 0, 2, 32:48]], axis=0)
        hi = jnp.concatenate([XB[dx, 1, 2, 0:16], XB[dx, 1, 2, 32:48]], axis=0)
        for isk in range(2):
            at = 8 * xl + 64 * isk
            mid = roll(main, 64) if isk else main
            out = jnp.where(
                l32b < 64, mid,
                jnp.where(l32b < 96, roll(hi, (192 - at) & 127), roll(lo, (248 - at) & 127)),
            )
            out = jnp.where(m, out, 0.0)
            if isk:
                L1.K[i, 8:40] = out
            else:
                L1.R[i] = out

    loop(0, 22, load1)
    L1.build()
    L1.smooth6()

    def up2(q):
        repeat_rows(T, repeat_lanes(L2.VB[q + 6, 12:28], 16), 16)
        for p in range(2):
            L1.VB[2 * q + 5 + p, 8:40] = L1.VB[2 * q + 5 + p, 8:40] + T[0:32]

    loop(0, 6, up2)

    ls, gsl, zz = group(48)

    def load_slab(xi):
        m = masks(xi + 1)
        x = 10 * gsl + (xi - 7)
        which = jnp.where(x >= 0, 1, 0) + jnp.where(x >= 16, 1, 0)
        xl = x & 15
        ilo = (8 * xl + zz) & 127
        ihi = (8 * xl + zz - 34) & 127
        imain = jnp.where(zz < 21, zz - 8, zz + 94) & 127
        for arr in range(2):
            src = L0.K if arr else L0.R
            parts = []
            for g in range(3):
                plane = src[10 * g + xi, 8:56] if arr else src[10 * g + xi]
                parts.append(gat(plane, imain))
            mid = jnp.where(gsl == 0, parts[0], jnp.where(gsl == 1, parts[1], parts[2]))
            lo = [gat(XB[d, 0, arr], ilo) for d in range(3)]
            hi = [gat(XB[d, 1, arr], ihi) for d in range(3)]
            pick = [jnp.where(which == 0, t[0], jnp.where(which == 1, t[1], t[2])) for t in (lo, hi)]
            out = jnp.where(zz < 8, pick[0], jnp.where(zz >= 34, pick[1], mid))
            out = jnp.where(m, out, 0.0)
            if arr:
                LS.K[1 + xi, 8:56] = out
            else:
                LS.R[1 + xi] = out

    loop(0, 10, load_slab)

    def ghosts(ref):
        ref[0, 8:56] = roll(ref[10, 8:56], 42)
        ref[11, 8:56] = roll(ref[1, 8:56], 86)

    ghosts(LS.K)
    LS.build()
    ghosts(LS.VA)
    LS.smooth6(after=ghosts, trim=False)

    l48, l24 = lanes(48), lanes(24)

    def merge(q):
        w = L1.VB[q + 6, 12:36]
        repeat_rows(T, gat(w, l24 >> 1), 24)
        repeat_rows(TH, gat(w, jnp.where(l24 == 0, 127, 64)), 24)
        for p in range(2):
            i = 2 * q + 5 + p
            g = jnp.where(i >= 10, 1, 0) + jnp.where(i >= 20, 1, 0)
            xi = i - 10 * g
            sv = LS.VB[1 + xi, 8:56]
            sk = LS.K[1 + xi, 8:56]
            off = 42 * g
            v = jnp.where(
                l48 < 6, roll(sv, (248 - off) & 127),
                jnp.where(l48 >= 122, roll(sv, (222 - off) & 127), L0.VB[i, 8:56]),
            )
            L0.VB[i, 8:56] = v + T[0:48]
            HV[i] = jnp.where(l48 < 64, roll(sv, (249 - off) & 127), roll(sv, (221 - off) & 127)) + TH[0:48]
            KH[i] = jnp.where(l48 < 64, roll(sk, (249 - off) & 127), roll(sk, (221 - off) & 127))

    loop(0, 10, merge)

    def final(x):
        i = x + 7
        c = slice(16, 48)
        v = L0.VB[i, c]
        k = L0.K[i, c]
        hv, kh = HV[i, 8:40], KH[i, 8:40]
        out = L0.CX[i, 8:40] * (v - L0.VB[i - 1, c])
        out = out + L0.CX[i + 1, 8:40] * (v - L0.VB[i + 1, c])
        out = out + L0.CY[i, 8:40] * (v - L0.VB[i, 15:47])
        out = out + L0.CY[i, 9:41] * (v - L0.VB[i, 17:49])
        cl = 0.5 * (k + jnp.where(l32 == 0, kh, roll(k, 1)))
        cr = 0.5 * (k + jnp.where(l32 == 127, kh, roll(k, 127)))
        out = out + cl * (v - jnp.where(l32 == 0, hv, roll(v, 1)))
        out = out + cr * (v - jnp.where(l32 == 127, hv, roll(v, 127)))
        corr_out[x] = v
        res_out[x] = r_in[x] - out

    loop(0, 16, final)

    each(gz > 0, zdown, "wait_send")
    each(gz < 7, zup, "wait_send")
    for ok, _, c in c0 + c1 + cx:
        each(ok, [c], "wait_send")
    for wide, thin, near, _ in gather:
        each(near, [wide], "wait_send")
        each(jnp.logical_not(near), [thin], "wait_send")
    for c in gather_z:
        c.wait_send()


def level_scratch(X, Y):
    big, mid = pltpu.VMEM((X, Y + 16, 128), f32), pltpu.VMEM((X, Y, 128), f32)
    return [big, mid, mid, pltpu.VMEM((X, Y + 8, 128), f32), mid, mid, big, big]


def shards(source, conductivity):
    dma = pltpu.SemaphoreType.DMA
    vm = lambda *shape: pltpu.VMEM(shape, f32)
    out = jax.ShapeDtypeStruct((16, 32, 128), f32)
    scratch = [
        vm(2, 30, 48, 128), vm(22, 32, 128), vm(32, 5, 8, 128), vm(3, 2, 3, 48, 128), vm(2, 3, 32, 128),
        vm(4, 8, 128), vm(48, 128), vm(48, 128), vm(8, 32, 128), vm(30, 48, 128), vm(30, 48, 128),
        dma((2,)), dma((8,)), dma((8,)), dma((8,)), dma((8,)), dma((31,)), dma((31,)), dma((2, 4)), dma((2, 4)),
        dma((8,)), dma((8,)), dma((31,)), dma((31,)),
    ]
    for X, Y in ((30, 48), (12, 48), (22, 32), (18, 24), (10, 32), (6, 16)):
        scratch += level_scratch(X, Y)
    return pl.pallas_call(
        kernel,
        out_shape=(out, out),
        in_specs=[pl.BlockSpec(memory_space=pltpu.VMEM)] * 2,
        out_specs=(pl.BlockSpec(memory_space=pltpu.VMEM),) * 2,
        scratch_shapes=scratch,
        compiler_params=pltpu.CompilerParams(
            collective_id=0, has_side_effects=True, vmem_limit_bytes=48 * 1024 * 1024
        ),
        name="multigrid",
    )(source, conductivity)


def solution(mesh):
    spec = P("gx", "gy", "gz")
    return jax.shard_map(shards, mesh=mesh, in_specs=(spec, spec), out_specs=(spec, spec), check_vma=False)
```

time: 928 us -> 102 us (0.11)
  the two profiles are of different devices: /device:TPU:31 before, /device:TPU:1 now
where the time goes in v1:
time: 102 us; the launch traced here: 101 us
  Pallas kernels  97.5 us (96%)
  local copies, waits for them, and re-layouts  3.3 us (3%)
    pallas_call x1, Pallas kernels, shards(): pl.pallas_call(kernel, out_shape=(out, out), in_specs=[pl.BlockSpec(memor...  97.5 us
    unnamed x6, local copies, waits for them, and re-layouts  3.3 us

profile of v1, /device:TPU:1, one launch (start us, length us, event | category | flops | bytes accessed | tf_op | source)
XLA Modules:
  0.0 101.4 jit_solution(14952089618941976517)
XLA Ops:
  0.6 0.0 copy-start
  0.6 0.9 copy-done
  1.6 0.0 copy-start.1
  1.6 0.9 copy-done.1
  2.5 97.5 %multigrid.1 = (f32[16,32,128]{2,1,0:T(8,128)S(1)}, f32[16,32,128]{2,1,0:T(8,128)S(1)}) custom-call(f32[16,32,128]{2,1,0:T(8,128)S(1)} %copy-done, f32[16,32,128]{2,1,0:T(8,128)S(1)} %copy-done.1), custom_call_target="tpu_custom_call" | custom-call | tf_op jit(solution)/shard_map/multigrid/pallas_call | solution.py:657
  100.0 0.7 copy.6
  100.7 0.7 copy.7
Async XLA Ops:
  0.6 1.0 copy-start
  1.6 0.9 copy-start.1

commit v2 on v1

--- a/solution.py
+++ b/solution.py
@@ -40,12 +40,23 @@
     return pltpu.roll(x, shift, 1)
 
 
-def loop(lo, hi, body):
-    def step(i, c):
-        body(i)
+def loop(lo, hi, width, body):
+    def chunk(first, count):
+        stores = [st for u in range(count) for st in body(first + u)]
+        for ref, index, value in stores:
+            ref[index] = value
+
+    def step(j, c):
+        chunk(lo + j * width, width)
         return c
 
-    lax.fori_loop(lo, hi, step, 0)
+    whole = (hi - lo) // width
+    if whole == 1:
+        chunk(lo, width)
+    elif whole > 1:
+        lax.fori_loop(0, whole, step, 0)
+    if (hi - lo) % width:
+        chunk(lo + whole * width, (hi - lo) % width)
 
 
 def rem(a, n):
@@ -53,8 +64,9 @@
 
 
 class Level:
-    def __init__(self, refs, planes, rows, factor, mask):
-        self.K, self.R, self.CX, self.CY, self.CZ, self.ID, self.VA, self.VB = refs
+    def __init__(self, refs, planes, rows, factor, mask, width):
+        self.K, self.R, self.CX, self.CY, self.CZ, self.CW, self.ID, self.VA, self.VB = refs
+        self.width = width
         self.X, self.Y, self.h, self.mask = planes, rows, 0.5 * factor, mask
 
     def clear(self):
@@ -62,11 +74,12 @@
         pad = jnp.zeros((8, 128), f32)
 
         def body(i):
+            out = []
             for ref in (self.K, self.VA, self.VB):
-                ref[i, 0:8] = pad
-                ref[i, 8 + Y : 16 + Y] = pad
-
-        loop(0, self.X, body)
+                out += [(ref, (i, slice(0, 8)), pad), (ref, (i, slice(8 + Y, 16 + Y)), pad)]
+            return out
+
+        loop(0, self.X, 6, body)
         full = jnp.zeros((Y, 128), f32)
         for i in (0, self.X - 1):
             for ref in (self.VA, self.VB, self.K):
@@ -79,19 +92,20 @@
             k = K[i, 8 : 8 + Y]
             low = h * (k + K[i - 1, 8 : 8 + Y])
             high = h * (k + K[i + 1, 8 : 8 + Y])
-            self.CX[i] = low
-            self.CX[i + 1] = high
-            self.CY[i] = h * (K[i, 8 : 16 + Y] + K[i, 7 : 15 + Y])
+            cy = h * (K[i, 8 : 16 + Y] + K[i, 7 : 15 + Y])
             cz = h * (k + roll(k, 1))
-            self.CZ[i] = cz
+            cw = h * (k + roll(k, 127))
             ylow = h * (k + K[i, 7 : 7 + Y])
             yhigh = h * (k + K[i, 9 : 9 + Y])
-            d = low + high + ylow + yhigh + cz + roll(cz, 127)
+            d = low + high + ylow + yhigh + cz + cw
             inv = jnp.where(self.mask(i), 1.0 / d, 0.0)
-            self.ID[i] = inv
-            self.VA[i, 8 : 8 + Y] = B0 * (self.R[i] * inv)
-
-        loop(1, self.X - 1, body)
+            first = B0 * (self.R[i] * inv)
+            return [
+                (self.CX, i, low), (self.CX, i + 1, high), (self.CY, i, cy), (self.CZ, i, cz), (self.CW, i, cw),
+                (self.ID, i, inv), (self.VA, (i, slice(8, 8 + Y)), first),
+            ]
+
+        loop(1, self.X - 1, self.width, body)
 
     def flux(self, V, i):
         Y = self.Y
@@ -100,8 +114,8 @@
         out = out + self.CX[i + 1] * (v - V[i + 1, 8 : 8 + Y])
         out = out + self.CY[i, 0:Y] * (v - V[i, 7 : 7 + Y])
         out = out + self.CY[i, 1 : 1 + Y] * (v - V[i, 9 : 9 + Y])
-        fz = self.CZ[i] * (v - roll(v, 1))
-        return v, out + (fz - roll(fz, 127))
+        out = out + self.CZ[i] * (v - roll(v, 1))
+        return v, out + self.CW[i] * (v - roll(v, 127))
 
     def step(self, src, dst, a, b, shrink, first=False):
         Y = self.Y
@@ -113,9 +127,9 @@
                 new = new + a * v
             elif a != 0.0:
                 new = new + a * (v - dst[i, 8 : 8 + Y])
-            dst[i, 8 : 8 + Y] = new
-
-        loop(1 + shrink, self.X - 1 - shrink, body)
+            return [(dst, (i, slice(8, 8 + Y)), new)]
+
+        loop(1 + shrink, self.X - 1 - shrink, self.width, body)
 
     def smooth6(self, after=None, trim=True):
         plan = [
@@ -192,12 +206,12 @@
     def mask4(i):
         return yz(16, 0, 16, 8, 8, 8)
 
-    L0 = Level(lv[0:8], 30, 48, 1.0, mask0)
-    LS = Level(lv[8:16], 12, 48, 1.0, masks)
-    L1 = Level(lv[16:24], 22, 32, 2.0, mask1)
-    L2 = Level(lv[24:32], 18, 24, 4.0, mask2)
-    L3 = Level(lv[32:40], 10, 32, 8.0, mask3)
-    L4 = Level(lv[40:48], 6, 16, 16.0, mask4)
+    L0 = Level(lv[0:9], 30, 48, 1.0, mask0, 2)
+    LS = Level(lv[9:18], 12, 48, 1.0, masks, 2)
+    L1 = Level(lv[18:27], 22, 32, 2.0, mask1, 3)
+    L2 = Level(lv[27:36], 18, 24, 4.0, mask2, 4)
+    L3 = Level(lv[36:45], 10, 32, 8.0, mask3, 4)
+    L4 = Level(lv[45:54], 6, 16, 16.0, mask4, 4)
 
     loc = [
         pltpu.make_async_copy(ref, E0.at[n, 7:23, 8:40], sem_loc.at[n]) for n, ref in enumerate((r_in, k_in))
@@ -218,7 +232,9 @@
             jnp.where(before, k8, c[3]),
         )
 
-    packed = lax.fori_loop(0, 16, pack0, (zero32,) * 4)
+    packed = (zero32,) * 4
+    for x in range(16):
+        packed = pack0(x, packed)
     PB[0, 0], PB[0, 1] = packed[0], packed[1]
     PB[1, 0], PB[1, 1] = roll(packed[2], 8), roll(packed[3], 8)
 
@@ -244,7 +260,9 @@
         )
 
     zero16 = jnp.zeros((16, 128), f32)
-    low1, high1 = lax.fori_loop(0, 8, down1, (zero16, zero16))
+    low1 = high1 = zero16
+    for x in range(8):
+        low1, high1 = down1(x, (low1, high1))
     for side, val in enumerate((low1, high1)):
         PB[side, 2, 0:8] = val[0:8]
         PB[side, 2, 24:32] = val[8:16]
@@ -268,15 +286,17 @@
             jnp.where(edge, roll(rk, (8 * x + 104) & 127), c[3]),
         )
 
-    r2, k2, low2, high2 = lax.fori_loop(0, 4, down2, (zero8,) * 4)
+    r2 = k2 = low2 = high2 = zero8
+    for x in range(4):
+        r2, k2, low2, high2 = down2(x, (r2, k2, low2, high2))
     l4 = lanes(4)
     rk3 = []
     for x in range(2):
         t = (RK2[2 * x, pl.ds(0, 4, stride=2)] + RK2[2 * x, pl.ds(1, 4, stride=2)]) + (
             RK2[2 * x + 1, pl.ds(0, 4, stride=2)] + RK2[2 * x + 1, pl.ds(1, 4, stride=2)]
         )
-        T[0:4], T[4:8] = t, t
-        t = pair(T[0:8], 8)
+        T[x, 0:4], T[x, 4:8] = t, t
+        t = pair(T[x, 0:8], 8)
         rk3.append(jnp.where(((l8 >> 4) & 1) == 1, 0.125 * t, t))
     m3 = jnp.where(((l8 >> 5) & 1) == 0, rk3[0], rk3[1])
     E23[own, 0], E23[own, 1], E23[own, 2] = r2, k2, m3
@@ -394,10 +414,11 @@
 
     def load0(i):
         m = mask0(i)
-        L0.K[i, 8:56] = jnp.where(m, E0[1, i], 0.0)
-        L0.R[i] = jnp.where(m, E0[0, i], 0.0)
-
-    loop(0, 30, load0)
+        return [
+            (L0.K, (i, slice(8, 56)), jnp.where(m, E0[1, i], 0.0)), (L0.R, i, jnp.where(m, E0[0, i], 0.0)),
+        ]
+
+    loop(0, 30, 3, load0)
     L0.build()
     L0.smooth6()
 
@@ -414,7 +435,7 @@
             m = jnp.where(top, E23[sa, 2], E23[sb, 2])
             lo = jnp.where(top, E23[sa, 3], E23[sb, 3])
             hi = jnp.where(top, E23[sa, 4], E23[sb, 4])
-            row = pl.multiple_of(8 * q, 8)
+            out3 = []
             for xl in range(2):
                 for isk in range(2):
                     at = 32 * xl + 16 * isk
@@ -423,33 +444,36 @@
                         jnp.where(l8 < 32, roll(hi, (16 - 64 - at) % 128), roll(lo, (112 - 64 - at) % 128)),
                     )
                     out = jnp.where(in3, out, 0.0)
+                    plane = 1 + 2 * sx + xl
                     if isk:
-                        L3.K[1 + 2 * sx + xl, pl.ds(8 + row, 8)] = out
+                        out3.append((L3.K, (plane, slice(8 + 8 * q, 16 + 8 * q)), out))
                     else:
-                        L3.R[1 + 2 * sx + xl, pl.ds(row, 8)] = out
-
-        loop(0, 4, load3)
+                        out3.append((L3.R, (plane, slice(8 * q, 8 * q + 8)), out))
+            return out3
+
+        loop(0, 4, 4, load3)
     L3.build()
     L3.step(L3.VA, L3.VB, A1, B1, 0, True)
 
     def residue(i):
         _, av = L3.flux(L3.VB, i)
-        RES[i - 1] = L3.R[i] - av
-
-    loop(1, 9, residue)
+        return [(RES, i - 1, L3.R[i] - av)]
+
+    loop(1, 9, 4, residue)
     in4 = mask4(0)
 
     def down4(x):
         t = (RES[2 * x, pl.ds(0, 16, stride=2)] + RES[2 * x, pl.ds(1, 16, stride=2)]) + (
             RES[2 * x + 1, pl.ds(0, 16, stride=2)] + RES[2 * x + 1, pl.ds(1, 16, stride=2)]
         )
-        L4.R[1 + x] = jnp.where(in4, pair(t, 16), 0.0)
+        r4 = jnp.where(in4, pair(t, 16), 0.0)
         t = (L3.K[1 + 2 * x, pl.ds(8, 16, stride=2)] + L3.K[1 + 2 * x, pl.ds(9, 16, stride=2)]) + (
             L3.K[2 + 2 * x, pl.ds(8, 16, stride=2)] + L3.K[2 + 2 * x, pl.ds(9, 16, stride=2)]
         )
-        L4.K[1 + x, 8:24] = jnp.where(in4, 0.125 * pair(t, 16), 0.0)
-
-    loop(0, 4, down4)
+        k4 = jnp.where(in4, 0.125 * pair(t, 16), 0.0)
+        return [(L4.R, 1 + x, r4), (L4.K, (1 + x, slice(8, 24)), k4)]
+
+    loop(0, 4, 4, down4)
     L4.build()
     L4.step(L4.VA, L4.VB, A1, B1, 0, True)
     L4.step(L4.VB, L4.VA, A2, B2, 0)
@@ -459,16 +483,17 @@
         l = lanes(rows)
         return gat(x, jnp.where(l < 96, l >> 1, (l >> 1) + 64))
 
-    def repeat_rows(ref, x, rows):
-        ref[pl.ds(0, rows, stride=2)] = x
-        ref[pl.ds(1, rows, stride=2)] = x
+    def repeat_rows(ref, slot, x, rows):
+        ref[slot, pl.ds(0, rows, stride=2)] = x
+        ref[slot, pl.ds(1, rows, stride=2)] = x
+        return ref[slot, 0 : 2 * rows]
 
     def up4(x):
-        repeat_rows(T, repeat_lanes(L4.VB[1 + x, 8:24], 16), 16)
-        for p in range(2):
-            L3.VB[1 + 2 * x + p, 8:40] = L3.VB[1 + 2 * x + p, 8:40] + T[0:32]
-
-    loop(0, 4, up4)
+        t = repeat_rows(T, x, repeat_lanes(L4.VB[1 + x, 8:24], 16), 16)
+        rows = slice(8, 40)
+        return [(L3.VB, (1 + 2 * x + p, rows), L3.VB[1 + 2 * x + p, rows] + t) for p in range(2)]
+
+    loop(0, 4, 4, up4)
     L3.step(L3.VB, L3.VA, 0.0, B0, 0)
     L3.step(L3.VA, L3.VB, A1, B1, 0)
 
@@ -478,6 +503,7 @@
         xl = xg & 3
         scx = jnp.clip(sx, 0, 3)
         m = mask2(i)
+        out2 = []
         for n in range(3):
             sy = jnp.clip(gy + n - 1, 0, 7)
             slot = scx * 8 + sy
@@ -491,21 +517,22 @@
                 )
                 out = jnp.where(mn, out, 0.0)
                 if isk:
-                    L2.K[i, 8 + 8 * n : 16 + 8 * n] = out
+                    out2.append((L2.K, (i, slice(8 + 8 * n, 16 + 8 * n)), out))
                 else:
-                    L2.R[i, 8 * n : 8 * n + 8] = out
-
-    loop(0, 18, load2)
+                    out2.append((L2.R, (i, slice(8 * n, 8 * n + 8)), out))
+        return out2
+
+    loop(0, 18, 3, load2)
     L2.build()
     L2.smooth6()
 
     def up3(q):
         w = L3.VB[2 * gx + q, pl.ds(4 * gy + 4, 16)]
-        repeat_rows(T, repeat_lanes(w, 16), 16)
-        for p in range(2):
-            L2.VB[2 * q + 5 + p, 8:32] = L2.VB[2 * q + 5 + p, 8:32] + T[0:24]
-
-    loop(0, 4, up3)
+        t = repeat_rows(T, 4 + q, repeat_lanes(w, 16), 16)[0:24]
+        rows = slice(8, 32)
+        return [(L2.VB, (2 * q + 5 + p, rows), L2.VB[2 * q + 5 + p, rows] + t) for p in range(2)]
+
+    loop(0, 4, 4, up3)
 
     for _, okr, c in c1:
         each(okr, [c], "wait_recv")
@@ -520,6 +547,7 @@
         xl = x & 7
         m = mask1(i)
         main = E1[i]
+        out1 = []
         lo = jnp.concatenate([XB[dx, 0, 2, 0:16], XB[dx, 0, 2, 32:48]], axis=0)
         hi = jnp.concatenate([XB[dx, 1, 2, 0:16], XB[dx, 1, 2, 32:48]], axis=0)
         for isk in range(2):
@@ -531,20 +559,21 @@
             )
             out = jnp.where(m, out, 0.0)
             if isk:
-                L1.K[i, 8:40] = out
+                out1.append((L1.K, (i, slice(8, 40)), out))
             else:
-                L1.R[i] = out
-
-    loop(0, 22, load1)
+                out1.append((L1.R, i, out))
+        return out1
+
+    loop(0, 22, 2, load1)
     L1.build()
     L1.smooth6()
 
     def up2(q):
-        repeat_rows(T, repeat_lanes(L2.VB[q + 6, 12:28], 16), 16)
-        for p in range(2):
-            L1.VB[2 * q + 5 + p, 8:40] = L1.VB[2 * q + 5 + p, 8:40] + T[0:32]
-
-    loop(0, 6, up2)
+        t = repeat_rows(T, 8 + q, repeat_lanes(L2.VB[q + 6, 12:28], 16), 16)
+        rows = slice(8, 40)
+        return [(L1.VB, (2 * q + 5 + p, rows), L1.VB[2 * q + 5 + p, rows] + t) for p in range(2)]
+
+    loop(0, 6, 6, up2)
 
     ls, gsl, zz = group(48)
 
@@ -556,6 +585,7 @@
         ilo = (8 * xl + zz) & 127
         ihi = (8 * xl + zz - 34) & 127
         imain = jnp.where(zz < 21, zz - 8, zz + 94) & 127
+        outs = []
         for arr in range(2):
             src = L0.K if arr else L0.R
             parts = []
@@ -569,11 +599,12 @@
             out = jnp.where(zz < 8, pick[0], jnp.where(zz >= 34, pick[1], mid))
             out = jnp.where(m, out, 0.0)
             if arr:
-                LS.K[1 + xi, 8:56] = out
+                outs.append((LS.K, (1 + xi, slice(8, 56)), out))
             else:
-                LS.R[1 + xi] = out
-
-    loop(0, 10, load_slab)
+                outs.append((LS.R, 1 + xi, out))
+        return outs
+
+    loop(0, 10, 1, load_slab)
 
     def ghosts(ref):
         ref[0, 8:56] = roll(ref[10, 8:56], 42)
@@ -588,8 +619,9 @@
 
     def merge(q):
         w = L1.VB[q + 6, 12:36]
-        repeat_rows(T, gat(w, l24 >> 1), 24)
-        repeat_rows(TH, gat(w, jnp.where(l24 == 0, 127, 64)), 24)
+        t = repeat_rows(T, 14 + q, gat(w, l24 >> 1), 24)
+        th = repeat_rows(TH, q, gat(w, jnp.where(l24 == 0, 127, 64)), 24)
+        out = []
         for p in range(2):
             i = 2 * q + 5 + p
             g = jnp.where(i >= 10, 1, 0) + jnp.where(i >= 20, 1, 0)
@@ -601,11 +633,12 @@
                 l48 < 6, roll(sv, (248 - off) & 127),
                 jnp.where(l48 >= 122, roll(sv, (222 - off) & 127), L0.VB[i, 8:56]),
             )
-            L0.VB[i, 8:56] = v + T[0:48]
-            HV[i] = jnp.where(l48 < 64, roll(sv, (249 - off) & 127), roll(sv, (221 - off) & 127)) + TH[0:48]
-            KH[i] = jnp.where(l48 < 64, roll(sk, (249 - off) & 127), roll(sk, (221 - off) & 127))
-
-    loop(0, 10, merge)
+            hv = jnp.where(l48 < 64, roll(sv, (249 - off) & 127), roll(sv, (221 - off) & 127)) + th
+            kh = jnp.where(l48 < 64, roll(sk, (249 - off) & 127), roll(sk, (221 - off) & 127))
+            out += [(L0.VB, (i, slice(8, 56)), v + t), (HV, i, hv), (KH, i, kh)]
+        return out
+
+    loop(0, 10, 1, merge)
 
     def final(x):
         i = x + 7
@@ -621,10 +654,9 @@
         cr = 0.5 * (k + jnp.where(l32 == 127, kh, roll(k, 127)))
         out = out + cl * (v - jnp.where(l32 == 0, hv, roll(v, 1)))
         out = out + cr * (v - jnp.where(l32 == 127, hv, roll(v, 127)))
-        corr_out[x] = v
-        res_out[x] = r_in[x] - out
-
-    loop(0, 16, final)
+        return [(corr_out, x, v), (res_out, x, r_in[x] - out)]
+
+    loop(0, 16, 2, final)
 
     each(gz > 0, zdown, "wait_send")
     each(gz < 7, zup, "wait_send")
@@ -639,7 +671,7 @@
 
 def level_scratch(X, Y):
     big, mid = pltpu.VMEM((X, Y + 16, 128), f32), pltpu.VMEM((X, Y, 128), f32)
-    return [big, mid, mid, pltpu.VMEM((X, Y + 8, 128), f32), mid, mid, big, big]
+    return [big, mid, mid, pltpu.VMEM((X, Y + 8, 128), f32), mid, mid, mid, big, big]
 
 
 def shards(source, conductivity):
@@ -648,7 +680,7 @@
     out = jax.ShapeDtypeStruct((16, 32, 128), f32)
     scratch = [
         vm(2, 30, 48, 128), vm(22, 32, 128), vm(32, 5, 8, 128), vm(3, 2, 3, 48, 128), vm(2, 3, 32, 128),
-        vm(4, 8, 128), vm(48, 128), vm(48, 128), vm(8, 32, 128), vm(30, 48, 128), vm(30, 48, 128),
+        vm(4, 8, 128), vm(24, 48, 128), vm(10, 48, 128), vm(8, 32, 128), vm(30, 48, 128), vm(30, 48, 128),
         dma((2,)), dma((8,)), dma((8,)), dma((8,)), dma((8,)), dma((31,)), dma((31,)), dma((2, 4)), dma((2, 4)),
         dma((8,)), dma((8,)), dma((31,)), dma((31,)),
     ]

time: 102 us -> 51.9 us (0.51)
  Pallas kernels: 97.5 us -> 47.9 us
    pallas_call x1, Pallas kernels: 97.5 us -> 47.9 us  [shards(): pl.pallas_call(kernel, out_shape=(out, out), in_specs=[pl.BlockSpec(memor...]
where the time goes in v2:
time: 51.9 us; the launch traced here: 51.8 us
  Pallas kernels  47.9 us (92%)
  local copies, waits for them, and re-layouts  3.3 us (6%)
  between operations  0.65 us (1%)
    pallas_call x1, Pallas kernels, shards(): pl.pallas_call(kernel, out_shape=(out, out), in_specs=[pl.BlockSpec(memor...  47.9 us
    unnamed x6, local copies, waits for them, and re-layouts  3.3 us

profile of v2, /device:TPU:1, one launch (start us, length us, event | category | flops | bytes accessed | tf_op | source)
XLA Modules:
  0.0 51.8 jit_solution(11570105768569734165)
XLA Ops:
  0.6 0.0 copy-start
  0.6 0.9 %copy-done = f32[16,32,128]{2,1,0:T(8,128)S(1)} copy-done((f32[16,32,128]{2,1,0:T(8,128)S(1)}, f32[16,32,128]{2,1,0:T(8,128)}, u32[]{:S(2)}) %copy-start) | copy-done | bytes 262168
  1.6 0.0 copy-start.1
  1.6 0.9 %copy-done.1 = f32[16,32,128]{2,1,0:T(8,128)S(1)} copy-done((f32[16,32,128]{2,1,0:T(8,128)S(1)}, f32[16,32,128]{2,1,0:T(8,128)}, u32[]{:S(2)}) %copy-start.1) | copy-done | bytes 262168
  2.5 47.9 %multigrid.1 = (f32[16,32,128]{2,1,0:T(8,128)S(1)}, f32[16,32,128]{2,1,0:T(8,128)S(1)}) custom-call(f32[16,32,128]{2,1,0:T(8,128)S(1)} %copy-done, f32[16,32,128]{2,1,0:T(8,128)S(1)} %copy-done.1), custom_call_target="tpu_custom_call" | custom-call | tf_op jit(solution)/shard_map/multigrid/pallas_call | solution.py:689
  50.4 0.7 %copy.6 = f32[16,32,128]{2,1,0:T(8,128)} copy(f32[16,32,128]{2,1,0:T(8,128)S(1)} %get-tuple-element.4) | data formatting | bytes 524288
  51.1 0.7 %copy.7 = f32[16,32,128]{2,1,0:T(8,128)} copy(f32[16,32,128]{2,1,0:T(8,128)S(1)} %get-tuple-element.5) | data formatting | bytes 524288
Async XLA Ops:
  0.6 1.0 %copy-start = (f32[16,32,128]{2,1,0:T(8,128)S(1)}, f32[16,32,128]{2,1,0:T(8,128)}, u32[]{:S(2)}) copy-start(f32[16,32,128]{2,1,0:T(8,128)} %r_in.1) | copy-start | bytes 786436
  1.6 0.9 %copy-start.1 = (f32[16,32,128]{2,1,0:T(8,128)S(1)}, f32[16,32,128]{2,1,0:T(8,128)}, u32[]{:S(2)}) copy-start(f32[16,32,128]{2,1,0:T(8,128)} %k_in.1) | copy-start | bytes 786436

commit v3 on v2

--- a/solution.py
+++ b/solution.py
@@ -21,7 +21,7 @@
 A3, B3 = W3 * W2, 2.0 * W3 / HALF
 
 NEAR = [(dx, dy) for dx in (-1, 0, 1) for dy in (-1, 0, 1) if (dx, dy) != (0, 0)]
-PLANE = [(a, b) for a in range(4) for b in range(8) if (a, b) != (0, 0)]
+DIAGONAL = [(dx, dy) for dx, dy in NEAR if dx * dy != 0]
 
 
 def lanes(rows):
@@ -146,26 +146,37 @@
 
 
 def kernel(r_in, k_in, corr_out, res_out, *s):
-    (E0, E1, E23, XB, PB, RK2, T, TH, RES, HV, KH, sem_loc, e0s, e0r, e1s, e1r, gs, gr, bs, br, xs, xr, cs, cr, *lv) = s
+    (E0, E1, E23, XB, PB, RK2, CB, T, TH, RES, HV, KH, sem_loc, e0s, e0r, e1s, e1r, gs, gr, bs, br, xs, xr, cs, cr, *lv) = s
     gx, gy, gz = lax.axis_index("gx"), lax.axis_index("gy"), lax.axis_index("gz")
-    own = gx * 8 + gy
+
+    loc = [
+        pltpu.make_async_copy(ref, E0.at[n, 7:23, 8:40], sem_loc.at[n]) for n, ref in enumerate((r_in, k_in))
+    ]
+    for c in loc:
+        c.start()
 
     bar = pltpu.get_barrier_semaphore()
 
-    def peer(a, b):
-        return rem(gx + a, 4), rem(gy + b, 8)
-
-    for a, b in PLANE:
-        px, py = peer(a, b)
-        pl.semaphore_signal(bar, inc=1, device_id={"gx": px, "gy": py}, device_id_type=MESH)
+    def inside(dx, dy):
+        return (gx + dx >= 0) & (gx + dx < 4) & (gy + dy >= 0) & (gy + dy < 8)
+
+    def greet(dev):
+        pl.semaphore_signal(bar, inc=1, device_id=dev, device_id_type=MESH)
+
+    for a in range(1, 4):
+        greet({"gx": rem(gx + a, 4)})
+    for b in range(1, 8):
+        greet({"gy": rem(gy + b, 8)})
+    for dx, dy in DIAGONAL:
+        pl.when(inside(dx, dy))(lambda dx=dx, dy=dy: greet({"gx": gx + dx, "gy": gy + dy}))
 
     @pl.when(gz > 0)
     def _():
-        pl.semaphore_signal(bar, inc=1, device_id={"gz": gz - 1}, device_id_type=MESH)
+        greet({"gz": gz - 1})
 
     @pl.when(gz < 7)
     def _():
-        pl.semaphore_signal(bar, inc=1, device_id={"gz": gz + 1}, device_id_type=MESH)
+        greet({"gz": gz + 1})
 
     def yz(rows, ylo, ny, zlo, zown, zhi):
         y = rowid(rows) + ylo
@@ -206,24 +217,21 @@
     def mask4(i):
         return yz(16, 0, 16, 8, 8, 8)
 
-    L0 = Level(lv[0:9], 30, 48, 1.0, mask0, 2)
-    LS = Level(lv[9:18], 12, 48, 1.0, masks, 2)
-    L1 = Level(lv[18:27], 22, 32, 2.0, mask1, 3)
-    L2 = Level(lv[27:36], 18, 24, 4.0, mask2, 4)
-    L3 = Level(lv[36:45], 10, 32, 8.0, mask3, 4)
+    L0 = Level(lv[0:9], 30, 48, 1.0, mask0, 8)
+    LS = Level(lv[9:18], 12, 48, 1.0, masks, 10)
+    L1 = Level(lv[18:27], 22, 32, 2.0, mask1, 10)
+    L2 = Level(lv[27:36], 18, 24, 4.0, mask2, 8)
+    L3 = Level(lv[36:45], 10, 32, 8.0, mask3, 8)
     L4 = Level(lv[45:54], 6, 16, 16.0, mask4, 4)
 
-    loc = [
-        pltpu.make_async_copy(ref, E0.at[n, 7:23, 8:40], sem_loc.at[n]) for n, ref in enumerate((r_in, k_in))
-    ]
     for c in loc:
-        c.start()
+        c.wait()
 
     l32 = lanes(32)
     zero32 = jnp.zeros((32, 128), f32)
 
     def pack0(x, c):
-        r8, k8 = roll(r_in[x], 8 * x), roll(k_in[x], 8 * x)
+        r8, k8 = (roll(E0[n, 7 + x, 8:40], 8 * x) for n in range(2))
         here, before = (l32 >> 3) == x, (l32 >> 3) == ((x + 15) & 15)
         return (
             jnp.where(here, r8, c[0]),
@@ -246,10 +254,9 @@
 
     def down1(x, c):
         out = []
-        for ref in (r_in, k_in):
-            t = (ref[2 * x, pl.ds(0, 16, stride=2)] + ref[2 * x, pl.ds(1, 16, stride=2)]) + (
-                ref[2 * x + 1, pl.ds(0, 16, stride=2)] + ref[2 * x + 1, pl.ds(1, 16, stride=2)]
-            )
+        for n in range(2):
+            a, b = (E0[n, 7 + 2 * x + p, pl.ds(8, 16, stride=2)] + E0[n, 7 + 2 * x + p, pl.ds(9, 16, stride=2)] for p in range(2))
+            t = a + b
             out.append(pair(t, 16))
         rk = jnp.where(l16 < 64, out[0], 0.125 * out[1])
         E1[7 + x, 8:24] = rk
@@ -299,23 +306,26 @@
         t = pair(T[x, 0:8], 8)
         rk3.append(jnp.where(((l8 >> 4) & 1) == 1, 0.125 * t, t))
     m3 = jnp.where(((l8 >> 5) & 1) == 0, rk3[0], rk3[1])
-    E23[own, 0], E23[own, 1], E23[own, 2] = r2, k2, m3
+    E23[gy, gx, 0], E23[gy, gx, 1] = r2, k2
     RK2[0] = jnp.where(l8 < 64, low2, m3)
     RK2[1] = jnp.where(l8 < 64, high2, m3)
 
     for L in (L0, LS, L1, L2, L3, L4):
         L.clear()
 
-    pl.semaphore_wait(bar, 31 + jnp.where(gz > 0, 1, 0) + jnp.where(gz < 7, 1, 0))
+    def sides(at, n):
+        return jnp.where(at > 0, 1, 0) + jnp.where(at < n - 1, 1, 0)
+
+    pl.semaphore_wait(bar, 10 + sides(gx, 4) * sides(gy, 8) + sides(gz, 8))
 
     def zcopies(side):
         dev = {"gz": gz - 1 if side == 0 else gz + 1}
         land = 1 - side
         pieces = [
-            (PB.at[side, 0:2], XB.at[1, land, 0:2, 8:40]),
+            (RK2.at[side], CB.at[land]),
             (PB.at[side, 2, 0:8], XB.at[1, land, 2, 8:16]),
             (PB.at[side, 2, 24:32], XB.at[1, land, 2, 32:40]),
-            (RK2.at[side], E23.at[own, 3 + land]),
+            (PB.at[side, 0:2], XB.at[1, land, 0:2, 8:40]),
         ]
         return [
             pltpu.make_async_remote_copy(
@@ -332,14 +342,8 @@
                 getattr(c, what)()
 
     zdown, zup = zcopies(0), zcopies(1)
-    each(gz > 0, zdown[::-1], "start")
-    each(gz < 7, zup[::-1], "start")
-
-    for c in loc:
-        c.wait()
-
-    def inside(dx, dy):
-        return (gx + dx >= 0) & (gx + dx < 4) & (gy + dy >= 0) & (gy + dy < 8)
+    each(gz > 0, zdown, "start")
+    each(gz < 7, zup, "start")
 
     SRC0X, DST0X = {-1: (7, 14), 0: (7, 23), 1: (16, 23)}, {-1: (23, 30), 0: (7, 23), 1: (0, 7)}
     SRC0Y, DST0Y = {-1: (8, 16), 0: (8, 40), 1: (32, 40)}, {-1: (40, 48), 0: (8, 40), 1: (0, 8)}
@@ -364,49 +368,59 @@
         E0.at[:, sl(SRC0X[dx]), sl(SRC0Y[dy])], E0.at[:, sl(DST0X[dx]), sl(DST0Y[dy])], e0s.at[n], e0r.at[n], dev_near(dx, dy)))
     c1 = near_copies(lambda n, dx, dy: rc(
         E1.at[sl(SRC1X[dx]), sl(SRC1Y[dy])], E1.at[sl(DST1X[dx]), sl(DST1Y[dy])], e1s.at[n], e1r.at[n], dev_near(dx, dy)))
-    cx = near_copies(lambda n, dx, dy: rc(
-        XB.at[1, :, :, sl(SRC0Y[dy])], XB.at[1 - dx, :, :, sl(DST0Y[dy])], xs.at[n], xr.at[n], dev_near(dx, dy)))
-
-    def close(a, b, sign):
-        px, py = rem(gx + sign * a + 4, 4), rem(gy + sign * b + 8, 8)
-        return (jnp.abs(px - gx) <= 2) & (jnp.abs(py - gy) <= 1)
-
-    gather, gather_z = [], []
-    for n, (a, b) in enumerate(PLANE):
-        px, py = peer(a, b)
-        dev = {"gx": px, "gy": py}
-        wide = rc(E23.at[own, 0:3], E23.at[own, 0:3], gs.at[n], gr.at[n], dev)
-        thin = rc(E23.at[own, 2:3], E23.at[own, 2:3], gs.at[n], gr.at[n], dev)
-        gather.append((wide, thin, close(a, b, 1), close(a, b, -1)))
-        gather_z.append(rc(E23.at[own, 3:5], E23.at[own, 3:5], cs.at[n], cr.at[n], dev))
-
-    for ok, _, c in c0:
+    def slab_copies(first, last, base):
+        return near_copies(lambda n, dx, dy: rc(
+            XB.at[1, :, first:last, sl(SRC0Y[dy])], XB.at[1 - dx, :, first:last, sl(DST0Y[dy])],
+            xs.at[base + n], xr.at[base + n], dev_near(dx, dy)))
+
+    cx1, cx0 = slab_copies(2, 3, 0), slab_copies(0, 2, 8)
+
+    gather_x = [
+        rc(E23.at[gy, gx], E23.at[gy, gx], gs.at[a - 1], gr.at[a - 1], {"gx": rem(gx + a, 4)}) for a in range(1, 4)
+    ]
+    gather_y = []
+    for b in range(1, 8):
+        dev = {"gy": rem(gy + b, 8)}
+        wide = rc(E23.at[gy], E23.at[gy], cs.at[b - 1], cr.at[b - 1], dev)
+        thin = rc(E23.at[gy, :, 3:4], E23.at[gy, :, 3:4], cs.at[b - 1], cr.at[b - 1], dev)
+        to = gy < 7 if b == 1 else gy > 0 if b == 7 else None
+        of = gy > 0 if b == 1 else gy < 7 if b == 7 else None
+        gather_y.append((wide, thin, to, of))
+
+    def each_y(what, end):
+        for wide, thin, to, of in gather_y:
+            cond = of if end else to
+            if cond is None:
+                getattr(thin, what)()
+            else:
+                each(cond, [wide], what)
+                each(jnp.logical_not(cond), [thin], what)
+
+    for ok, _, c in c0 + c1:
         each(ok, [c], "start")
-    for ok, _, c in c1:
-        each(ok, [c], "start")
-    for wide, thin, near, _ in gather:
-        each(near, [wide], "start")
-        each(jnp.logical_not(near), [thin], "start")
 
     @pl.when(gz == 0)
     def _():
         for n in range(3):
             XB[1, 0, n, 8:40] = zero32
-        E23[own, 3] = zero8
+        CB[0] = zero8
 
     @pl.when(gz == 7)
     def _():
         for n in range(3):
             XB[1, 1, n, 8:40] = zero32
-        E23[own, 4] = zero8
-
-    each(gz < 7, [zdown[3]], "wait_recv")
-    each(gz > 0, [zup[3]], "wait_recv")
-    for c in gather_z:
+        CB[1] = zero8
+
+    each(gz < 7, zdown[0:1], "wait_recv")
+    each(gz > 0, zup[0:1], "wait_recv")
+    top = rowid(8) < 4
+    E23[gy, gx, 2] = jnp.where(l8 < 64, CB[0], roll(CB[1], 64))
+    E23[gy, gx, 3] = jnp.where(l8 < 64, m3, jnp.where(top, CB[0], CB[1]))
+    for c in gather_x:
         c.start()
-    each(gz < 7, zdown[0:3], "wait_recv")
-    each(gz > 0, zup[0:3], "wait_recv")
-    for ok, _, c in cx:
+    each(gz < 7, zdown[1:3], "wait_recv")
+    each(gz > 0, zup[1:3], "wait_recv")
+    for ok, _, c in cx1:
         each(ok, [c], "start")
 
     for _, okr, c in c0:
@@ -418,23 +432,25 @@
             (L0.K, (i, slice(8, 56)), jnp.where(m, E0[1, i], 0.0)), (L0.R, i, jnp.where(m, E0[0, i], 0.0)),
         ]
 
-    loop(0, 30, 3, load0)
+    loop(0, 30, 6, load0)
     L0.build()
+    for c in gather_x:
+        c.wait_recv()
+    each_y("start", False)
+    each(gz < 7, zdown[3:4], "wait_recv")
+    each(gz > 0, zup[3:4], "wait_recv")
+    for ok, _, c in cx0:
+        each(ok, [c], "start")
     L0.smooth6()
 
-    for wide, thin, _, near in gather:
-        each(near, [wide], "wait_recv")
-        each(jnp.logical_not(near), [thin], "wait_recv")
-    for c in gather_z:
-        c.wait_recv()
-    top = rowid(8) < 4
+    each_y("wait_recv", True)
     in3 = yz(8, 0, 8, 16, 16, 16)
     for sx in range(4):
         def load3(q, sx=sx):
-            sa, sb = sx * 8 + 2 * q, sx * 8 + 2 * q + 1
-            m = jnp.where(top, E23[sa, 2], E23[sb, 2])
-            lo = jnp.where(top, E23[sa, 3], E23[sb, 3])
-            hi = jnp.where(top, E23[sa, 4], E23[sb, 4])
+            a, b = E23[2 * q, sx, 3], E23[2 * q + 1, sx, 3]
+            m = jnp.where(top, a, b)
+            lo = jnp.where(top, a, pltpu.roll(b, 4, 0))
+            hi = jnp.where(top, pltpu.roll(a, 4, 0), b)
             out3 = []
             for xl in range(2):
                 for isk in range(2):
@@ -506,14 +522,13 @@
         out2 = []
         for n in range(3):
             sy = jnp.clip(gy + n - 1, 0, 7)
-            slot = scx * 8 + sy
-            r, k, lo, hi = E23[slot, 0], E23[slot, 1], E23[slot, 3], E23[slot, 4]
+            r, k, edge = E23[sy, scx, 0], E23[sy, scx, 1], E23[sy, scx, 2]
             mn = m[8 * n : 8 * n + 8]
             for isk, mid in ((0, r), (1, k)):
                 at = 8 * xl + 32 * isk
                 out = jnp.where(
                     l8 < 32, roll(mid, (128 - 32 * xl) & 127),
-                    jnp.where(l8 < 64, roll(hi, (160 - at) & 127), roll(lo, (248 - at) & 127)),
+                    jnp.where(l8 < 64, roll(edge, (224 - at) & 127), roll(edge, (248 - at) & 127)),
                 )
                 out = jnp.where(mn, out, 0.0)
                 if isk:
@@ -522,7 +537,7 @@
                     out2.append((L2.R, (i, slice(8 * n, 8 * n + 8)), out))
         return out2
 
-    loop(0, 18, 3, load2)
+    loop(0, 18, 6, load2)
     L2.build()
     L2.smooth6()
 
@@ -534,9 +549,7 @@
 
     loop(0, 4, 4, up3)
 
-    for _, okr, c in c1:
-        each(okr, [c], "wait_recv")
-    for _, okr, c in cx:
+    for _, okr, c in c1 + cx1:
         each(okr, [c], "wait_recv")
 
     l32b = lanes(32)
@@ -564,7 +577,7 @@
                 out1.append((L1.R, i, out))
         return out1
 
-    loop(0, 22, 2, load1)
+    loop(0, 22, 4, load1)
     L1.build()
     L1.smooth6()
 
@@ -575,6 +588,8 @@
 
     loop(0, 6, 6, up2)
 
+    for _, okr, c in cx0:
+        each(okr, [c], "wait_recv")
     ls, gsl, zz = group(48)
 
     def load_slab(xi):
@@ -604,7 +619,7 @@
                 outs.append((LS.R, 1 + xi, out))
         return outs
 
-    loop(0, 10, 1, load_slab)
+    loop(0, 10, 2, load_slab)
 
     def ghosts(ref):
         ref[0, 8:56] = roll(ref[10, 8:56], 42)
@@ -638,7 +653,7 @@
             out += [(L0.VB, (i, slice(8, 56)), v + t), (HV, i, hv), (KH, i, kh)]
         return out
 
-    loop(0, 10, 1, merge)
+    loop(0, 10, 2, merge)
 
     def final(x):
         i = x + 7
@@ -654,19 +669,17 @@
         cr = 0.5 * (k + jnp.where(l32 == 127, kh, roll(k, 127)))
         out = out + cl * (v - jnp.where(l32 == 0, hv, roll(v, 1)))
         out = out + cr * (v - jnp.where(l32 == 127, hv, roll(v, 127)))
-        return [(corr_out, x, v), (res_out, x, r_in[x] - out)]
-
-    loop(0, 16, 2, final)
+        return [(corr_out, x, v), (res_out, x, E0[0, i, 8:40] - out)]
+
+    loop(0, 16, 4, final)
 
     each(gz > 0, zdown, "wait_send")
     each(gz < 7, zup, "wait_send")
-    for ok, _, c in c0 + c1 + cx:
+    for ok, _, c in c0 + c1 + cx0 + cx1:
         each(ok, [c], "wait_send")
-    for wide, thin, near, _ in gather:
-        each(near, [wide], "wait_send")
-        each(jnp.logical_not(near), [thin], "wait_send")
-    for c in gather_z:
+    for c in gather_x:
         c.wait_send()
+    each_y("wait_send", False)
 
 
 def level_scratch(X, Y):
@@ -679,17 +692,17 @@
     vm = lambda *shape: pltpu.VMEM(shape, f32)
     out = jax.ShapeDtypeStruct((16, 32, 128), f32)
     scratch = [
-        vm(2, 30, 48, 128), vm(22, 32, 128), vm(32, 5, 8, 128), vm(3, 2, 3, 48, 128), vm(2, 3, 32, 128),
-        vm(4, 8, 128), vm(24, 48, 128), vm(10, 48, 128), vm(8, 32, 128), vm(30, 48, 128), vm(30, 48, 128),
-        dma((2,)), dma((8,)), dma((8,)), dma((8,)), dma((8,)), dma((31,)), dma((31,)), dma((2, 4)), dma((2, 4)),
-        dma((8,)), dma((8,)), dma((31,)), dma((31,)),
+        vm(2, 30, 48, 128), vm(22, 32, 128), vm(8, 4, 4, 8, 128), vm(3, 2, 3, 48, 128), vm(2, 3, 32, 128),
+        vm(4, 8, 128), vm(2, 8, 128), vm(24, 48, 128), vm(10, 48, 128), vm(8, 32, 128), vm(30, 48, 128), vm(30, 48, 128),
+        dma((2,)), dma((8,)), dma((8,)), dma((8,)), dma((8,)), dma((3,)), dma((3,)), dma((2, 4)), dma((2, 4)),
+        dma((16,)), dma((16,)), dma((7,)), dma((7,)),
     ]
     for X, Y in ((30, 48), (12, 48), (22, 32), (18, 24), (10, 32), (6, 16)):
         scratch += level_scratch(X, Y)
     return pl.pallas_call(
         kernel,
         out_shape=(out, out),
-        in_specs=[pl.BlockSpec(memory_space=pltpu.VMEM)] * 2,
+        in_specs=[pl.BlockSpec(memory_space=pltpu.HBM)] * 2,
         out_specs=(pl.BlockSpec(memory_space=pltpu.VMEM),) * 2,
         scratch_shapes=scratch,
         compiler_params=pltpu.CompilerParams(

time: 51.9 us -> 42.2 us (0.81)
  Pallas kernels: 47.9 us -> 38.1 us
    pallas_call x1, Pallas kernels: 47.9 us -> 38.1 us  [shards(): pl.pallas_call(kernel, out_shape=(out, out), in_specs=[pl.BlockSpec(memor...]
where the time goes in v3:
time: 42.2 us; the launch traced here: 42 us
  Pallas kernels  38.1 us (90%)
  local copies, waits for them, and re-layouts  3.3 us (8%)
  between operations  0.65 us (2%)
    pallas_call x1, Pallas kernels, shards(): pl.pallas_call(kernel, out_shape=(out, out), in_specs=[pl.BlockSpec(memor...  38.1 us
    unnamed x6, local copies, waits for them, and re-layouts  3.3 us

profile of v3, /device:TPU:1, one launch (start us, length us, event | category | flops | bytes accessed | tf_op | source)
XLA Modules:
  0.0 42.0 jit_solution(4624111739799185901)
XLA Ops:
  0.6 0.0 copy-start
  0.6 0.9 %copy-done = f32[16,32,128]{2,1,0:T(8,128)S(1)} copy-done((f32[16,32,128]{2,1,0:T(8,128)S(1)}, f32[16,32,128]{2,1,0:T(8,128)}, u32[]{:S(2)}) %copy-start) | copy-done | bytes 262168
  1.6 0.0 copy-start.1
  1.6 0.9 %copy-done.1 = f32[16,32,128]{2,1,0:T(8,128)S(1)} copy-done((f32[16,32,128]{2,1,0:T(8,128)S(1)}, f32[16,32,128]{2,1,0:T(8,128)}, u32[]{:S(2)}) %copy-start.1) | copy-done | bytes 262168
  2.5 38.1 %multigrid.1 = (f32[16,32,128]{2,1,0:T(8,128)S(1)}, f32[16,32,128]{2,1,0:T(8,128)S(1)}) custom-call(f32[16,32,128]{2,1,0:T(8,128)S(1)} %copy-done, f32[16,32,128]{2,1,0:T(8,128)S(1)} %copy-done.1), custom_call_target="tpu_custom_call" | custom-call | tf_op jit(solution)/shard_map/multigrid/pallas_call | solution.py:702
  40.6 0.7 %copy.6 = f32[16,32,128]{2,1,0:T(8,128)} copy(f32[16,32,128]{2,1,0:T(8,128)S(1)} %get-tuple-element.4) | data formatting | bytes 524288
  41.3 0.7 %copy.7 = f32[16,32,128]{2,1,0:T(8,128)} copy(f32[16,32,128]{2,1,0:T(8,128)S(1)} %get-tuple-element.5) | data formatting | bytes 524288
Async XLA Ops:
  0.6 1.0 %copy-start = (f32[16,32,128]{2,1,0:T(8,128)S(1)}, f32[16,32,128]{2,1,0:T(8,128)}, u32[]{:S(2)}) copy-start(f32[16,32,128]{2,1,0:T(8,128)} %r_in.1) | copy-start | bytes 786436
  1.6 0.9 %copy-start.1 = (f32[16,32,128]{2,1,0:T(8,128)S(1)}, f32[16,32,128]{2,1,0:T(8,128)}, u32[]{:S(2)}) copy-start(f32[16,32,128]{2,1,0:T(8,128)} %k_in.1) | copy-start | bytes 786436

commit v4 on v3

--- a/solution.py
+++ b/solution.py
@@ -163,20 +163,20 @@
     def greet(dev):
         pl.semaphore_signal(bar, inc=1, device_id=dev, device_id_type=MESH)
 
+    @pl.when(gz > 0)
+    def _():
+        greet({"gz": gz - 1})
+
+    @pl.when(gz < 7)
+    def _():
+        greet({"gz": gz + 1})
+
     for a in range(1, 4):
         greet({"gx": rem(gx + a, 4)})
     for b in range(1, 8):
         greet({"gy": rem(gy + b, 8)})
     for dx, dy in DIAGONAL:
         pl.when(inside(dx, dy))(lambda dx=dx, dy=dy: greet({"gx": gx + dx, "gy": gy + dy}))
-
-    @pl.when(gz > 0)
-    def _():
-        greet({"gz": gz - 1})
-
-    @pl.when(gz < 7)
-    def _():
-        greet({"gz": gz + 1})
 
     def yz(rows, ylo, ny, zlo, zown, zhi):
         y = rowid(rows) + ylo
@@ -364,10 +364,15 @@
     def dev_near(dx, dy):
         return {"gx": gx + dx, "gy": gy + dy}
 
+    def thinner(pairs, dx, dy):
+        if dx == 0 or dy == 0:
+            return sl(pairs)
+        return sl((pairs[0] + 1, pairs[1])) if dx == 1 else sl((pairs[0], pairs[1] - 1))
+
     c0 = near_copies(lambda n, dx, dy: rc(
-        E0.at[:, sl(SRC0X[dx]), sl(SRC0Y[dy])], E0.at[:, sl(DST0X[dx]), sl(DST0Y[dy])], e0s.at[n], e0r.at[n], dev_near(dx, dy)))
+        E0.at[:, thinner(SRC0X[dx], dx, dy), sl(SRC0Y[dy])], E0.at[:, thinner(DST0X[dx], dx, dy), sl(DST0Y[dy])], e0s.at[n], e0r.at[n], dev_near(dx, dy)))
     c1 = near_copies(lambda n, dx, dy: rc(
-        E1.at[sl(SRC1X[dx]), sl(SRC1Y[dy])], E1.at[sl(DST1X[dx]), sl(DST1Y[dy])], e1s.at[n], e1r.at[n], dev_near(dx, dy)))
+        E1.at[thinner(SRC1X[dx], dx, dy), sl(SRC1Y[dy])], E1.at[thinner(DST1X[dx], dx, dy), sl(DST1Y[dy])], e1s.at[n], e1r.at[n], dev_near(dx, dy)))
     def slab_copies(first, last, base):
         return near_copies(lambda n, dx, dy: rc(
             XB.at[1, :, first:last, sl(SRC0Y[dy])], XB.at[1 - dx, :, first:last, sl(DST0Y[dy])],
@@ -396,7 +401,7 @@
                 each(cond, [wide], what)
                 each(jnp.logical_not(cond), [thin], what)
 
-    for ok, _, c in c0 + c1:
+    for ok, _, c in c1 + [c0[1], c0[6], c0[3], c0[4], c0[0], c0[2], c0[5], c0[7]]:
         each(ok, [c], "start")
 
     @pl.when(gz == 0)
@@ -423,17 +428,6 @@
     for ok, _, c in cx1:
         each(ok, [c], "start")
 
-    for _, okr, c in c0:
-        each(okr, [c], "wait_recv")
-
-    def load0(i):
-        m = mask0(i)
-        return [
-            (L0.K, (i, slice(8, 56)), jnp.where(m, E0[1, i], 0.0)), (L0.R, i, jnp.where(m, E0[0, i], 0.0)),
-        ]
-
-    loop(0, 30, 6, load0)
-    L0.build()
     for c in gather_x:
         c.wait_recv()
     each_y("start", False)
@@ -441,6 +435,50 @@
     each(gz > 0, zup[3:4], "wait_recv")
     for ok, _, c in cx0:
         each(ok, [c], "start")
+
+    for _, okr, c in c1 + cx1:
+        each(okr, [c], "wait_recv")
+
+    l32b = lanes(32)
+
+    def load1(i):
+        x = i - 7
+        dx = jnp.where(x >= 0, 1, 0) + jnp.where(x >= 8, 1, 0)
+        xl = x & 7
+        m = mask1(i)
+        main = E1[i]
+        out1 = []
+        lo = jnp.concatenate([XB[dx, 0, 2, 0:16], XB[dx, 0, 2, 32:48]], axis=0)
+        hi = jnp.concatenate([XB[dx, 1, 2, 0:16], XB[dx, 1, 2, 32:48]], axis=0)
+        for isk in range(2):
+            at = 8 * xl + 64 * isk
+            mid = roll(main, 64) if isk else main
+            out = jnp.where(
+                l32b < 64, mid,
+                jnp.where(l32b < 96, roll(hi, (192 - at) & 127), roll(lo, (248 - at) & 127)),
+            )
+            out = jnp.where(m, out, 0.0)
+            if isk:
+                out1.append((L1.K, (i, slice(8, 40)), out))
+            else:
+                out1.append((L1.R, i, out))
+        return out1
+
+    loop(0, 22, 4, load1)
+    L1.build()
+    L1.smooth6()
+
+    for _, okr, c in c0:
+        each(okr, [c], "wait_recv")
+
+    def load0(i):
+        m = mask0(i)
+        return [
+            (L0.K, (i, slice(8, 56)), jnp.where(m, E0[1, i], 0.0)), (L0.R, i, jnp.where(m, E0[0, i], 0.0)),
+        ]
+
+    loop(0, 30, 6, load0)
+    L0.build()
     L0.smooth6()
 
     each_y("wait_recv", True)
@@ -548,38 +586,6 @@
         return [(L2.VB, (2 * q + 5 + p, rows), L2.VB[2 * q + 5 + p, rows] + t) for p in range(2)]
 
     loop(0, 4, 4, up3)
-
-    for _, okr, c in c1 + cx1:
-        each(okr, [c], "wait_recv")
-
-    l32b = lanes(32)
-
-    def load1(i):
-        x = i - 7
-        dx = jnp.where(x >= 0, 1, 0) + jnp.where(x >= 8, 1, 0)
-        xl = x & 7
-        m = mask1(i)
-        main = E1[i]
-        out1 = []
-        lo = jnp.concatenate([XB[dx, 0, 2, 0:16], XB[dx, 0, 2, 32:48]], axis=0)
-        hi = jnp.concatenate([XB[dx, 1, 2, 0:16], XB[dx, 1, 2, 32:48]], axis=0)
-        for isk in range(2):
-            at = 8 * xl + 64 * isk
-            mid = roll(main, 64) if isk else main
-            out = jnp.where(
-                l32b < 64, mid,
-                jnp.where(l32b < 96, roll(hi, (192 - at) & 127), roll(lo, (248 - at) & 127)),
-            )
-            out = jnp.where(m, out, 0.0)
-            if isk:
-                out1.append((L1.K, (i, slice(8, 40)), out))
-            else:
-                out1.append((L1.R, i, out))
-        return out1
-
-    loop(0, 22, 4, load1)
-    L1.build()
-    L1.smooth6()
 
     def up2(q):
         t = repeat_rows(T, 8 + q, repeat_lanes(L2.VB[q + 6, 12:28], 16), 16)

time: 42.2 us -> 40.2 us (0.953)
  Pallas kernels: 38.1 us -> 35.8 us
    pallas_call x1, Pallas kernels: 38.1 us -> 35.8 us  [shards(): pl.pallas_call(kernel, out_shape=(out, out), in_specs=[pl.BlockSpec(memor...]
where the time goes in v4:
time: 40.2 us; the launch traced here: 39.8 us
  Pallas kernels  35.8 us (89%)
  local copies, waits for them, and re-layouts  3.3 us (8%)
  between operations  0.65 us (2%)
    pallas_call x1, Pallas kernels, shards(): pl.pallas_call(kernel, out_shape=(out, out), in_specs=[pl.BlockSpec(memor...  35.8 us
    unnamed x6, local copies, waits for them, and re-layouts  3.3 us

profile of v4, /device:TPU:1, one launch (start us, length us, event | category | flops | bytes accessed | tf_op | source)
XLA Modules:
  0.0 39.8 jit_solution(9872795964959356337)
XLA Ops:
  0.6 0.0 copy-start
  0.6 0.9 %copy-done = f32[16,32,128]{2,1,0:T(8,128)S(1)} copy-done((f32[16,32,128]{2,1,0:T(8,128)S(1)}, f32[16,32,128]{2,1,0:T(8,128)}, u32[]{:S(2)}) %copy-start) | copy-done | bytes 262168
  1.6 0.0 copy-start.1
  1.6 0.9 %copy-done.1 = f32[16,32,128]{2,1,0:T(8,128)S(1)} copy-done((f32[16,32,128]{2,1,0:T(8,128)S(1)}, f32[16,32,128]{2,1,0:T(8,128)}, u32[]{:S(2)}) %copy-start.1) | copy-done | bytes 262168
  2.5 35.8 %multigrid.1 = (f32[16,32,128]{2,1,0:T(8,128)S(1)}, f32[16,32,128]{2,1,0:T(8,128)S(1)}) custom-call(f32[16,32,128]{2,1,0:T(8,128)S(1)} %copy-done, f32[16,32,128]{2,1,0:T(8,128)S(1)} %copy-done.1), custom_call_target="tpu_custom_call" | custom-call | tf_op jit(solution)/shard_map/multigrid/pallas_call | solution.py:708
  38.4 0.7 %copy.6 = f32[16,32,128]{2,1,0:T(8,128)} copy(f32[16,32,128]{2,1,0:T(8,128)S(1)} %get-tuple-element.4) | data formatting | bytes 524288
  39.1 0.7 %copy.7 = f32[16,32,128]{2,1,0:T(8,128)} copy(f32[16,32,128]{2,1,0:T(8,128)S(1)} %get-tuple-element.5) | data formatting | bytes 524288
Async XLA Ops:
  0.6 1.0 %copy-start = (f32[16,32,128]{2,1,0:T(8,128)S(1)}, f32[16,32,128]{2,1,0:T(8,128)}, u32[]{:S(2)}) copy-start(f32[16,32,128]{2,1,0:T(8,128)} %r_in.1) | copy-start | bytes 786436
  1.6 0.9 %copy-start.1 = (f32[16,32,128]{2,1,0:T(8,128)S(1)}, f32[16,32,128]{2,1,0:T(8,128)}, u32[]{:S(2)}) copy-start(f32[16,32,128]{2,1,0:T(8,128)} %k_in.1) | copy-start | bytes 786436

commit v5 on v4

--- a/solution.py
+++ b/solution.py
@@ -85,7 +85,7 @@
             for ref in (self.VA, self.VB, self.K):
                 ref[i, 8 : 8 + Y] = full
 
-    def build(self):
+    def build(self, start=True):
         Y, h, K = self.Y, self.h, self.K
 
         def body(i):
@@ -99,10 +99,10 @@
             yhigh = h * (k + K[i, 9 : 9 + Y])
             d = low + high + ylow + yhigh + cz + cw
             inv = jnp.where(self.mask(i), 1.0 / d, 0.0)
-            first = B0 * (self.R[i] * inv)
-            return [
+            first = [(self.VA, (i, slice(8, 8 + Y)), B0 * (self.R[i] * inv))] if start else []
+            return first + [
                 (self.CX, i, low), (self.CX, i + 1, high), (self.CY, i, cy), (self.CZ, i, cz), (self.CW, i, cw),
-                (self.ID, i, inv), (self.VA, (i, slice(8, 8 + Y)), first),
+                (self.ID, i, inv),
             ]
 
         loop(1, self.X - 1, self.width, body)
@@ -369,8 +369,12 @@
             return sl(pairs)
         return sl((pairs[0] + 1, pairs[1])) if dx == 1 else sl((pairs[0], pairs[1] - 1))
 
-    c0 = near_copies(lambda n, dx, dy: rc(
-        E0.at[:, thinner(SRC0X[dx], dx, dy), sl(SRC0Y[dy])], E0.at[:, thinner(DST0X[dx], dx, dy), sl(DST0Y[dy])], e0s.at[n], e0r.at[n], dev_near(dx, dy)))
+    def fine(arr):
+        return near_copies(lambda n, dx, dy: rc(
+            E0.at[arr, thinner(SRC0X[dx], dx, dy), sl(SRC0Y[dy])], E0.at[arr, thinner(DST0X[dx], dx, dy), sl(DST0Y[dy])],
+            e0s.at[8 * arr + n], e0r.at[8 * arr + n], dev_near(dx, dy)))
+
+    c0r, c0k = fine(0), fine(1)
     c1 = near_copies(lambda n, dx, dy: rc(
         E1.at[thinner(SRC1X[dx], dx, dy), sl(SRC1Y[dy])], E1.at[thinner(DST1X[dx], dx, dy), sl(DST1Y[dy])], e1s.at[n], e1r.at[n], dev_near(dx, dy)))
     def slab_copies(first, last, base):
@@ -388,20 +392,23 @@
         dev = {"gy": rem(gy + b, 8)}
         wide = rc(E23.at[gy], E23.at[gy], cs.at[b - 1], cr.at[b - 1], dev)
         thin = rc(E23.at[gy, :, 3:4], E23.at[gy, :, 3:4], cs.at[b - 1], cr.at[b - 1], dev)
-        to = gy < 7 if b == 1 else gy > 0 if b == 7 else None
-        of = gy > 0 if b == 1 else gy < 7 if b == 7 else None
-        gather_y.append((wide, thin, to, of))
+        up, fromlow = gy + b < 8, gy - b >= 0
+        if b == 4:
+            gather_y.append((thin, None, None))
+        elif b < 4:
+            gather_y.append((wide if b == 1 else thin, up, fromlow))
+        else:
+            gather_y.append((wide if b == 7 else thin, jnp.logical_not(up), jnp.logical_not(fromlow)))
 
     def each_y(what, end):
-        for wide, thin, to, of in gather_y:
+        for copy, to, of in gather_y:
             cond = of if end else to
             if cond is None:
-                getattr(thin, what)()
+                getattr(copy, what)()
             else:
-                each(cond, [wide], what)
-                each(jnp.logical_not(cond), [thin], what)
-
-    for ok, _, c in c1 + [c0[1], c0[6], c0[3], c0[4], c0[0], c0[2], c0[5], c0[7]]:
+                each(cond, [copy], what)
+
+    for ok, _, c in c1 + [c0k[n] for n in (1, 6, 3, 4, 0, 2, 5, 7)]:
         each(ok, [c], "start")
 
     @pl.when(gz == 0)
@@ -425,7 +432,7 @@
         c.start()
     each(gz < 7, zdown[1:3], "wait_recv")
     each(gz > 0, zup[1:3], "wait_recv")
-    for ok, _, c in cx1:
+    for ok, _, c in cx1 + [c0r[n] for n in (1, 6, 3, 4, 0, 2, 5, 7)]:
         each(ok, [c], "start")
 
     for c in gather_x:
@@ -468,131 +475,19 @@
     L1.build()
     L1.smooth6()
 
-    for _, okr, c in c0:
+    for _, okr, c in c0k:
         each(okr, [c], "wait_recv")
+    loop(0, 30, 6, lambda i: [(L0.K, (i, slice(8, 56)), jnp.where(mask0(i), E0[1, i], 0.0))])
+    L0.build(start=False)
+    for _, okr, c in c0r:
+        each(okr, [c], "wait_recv")
 
     def load0(i):
-        m = mask0(i)
-        return [
-            (L0.K, (i, slice(8, 56)), jnp.where(m, E0[1, i], 0.0)), (L0.R, i, jnp.where(m, E0[0, i], 0.0)),
-        ]
-
-    loop(0, 30, 6, load0)
-    L0.build()
+        r = jnp.where(mask0(i), E0[0, i], 0.0)
+        return [(L0.R, i, r), (L0.VA, (i, slice(8, 56)), B0 * (r * L0.ID[i]))]
+
+    loop(1, 29, 7, load0)
     L0.smooth6()
-
-    each_y("wait_recv", True)
-    in3 = yz(8, 0, 8, 16, 16, 16)
-    for sx in range(4):
-        def load3(q, sx=sx):
-            a, b = E23[2 * q, sx, 3], E23[2 * q + 1, sx, 3]
-            m = jnp.where(top, a, b)
-            lo = jnp.where(top, a, pltpu.roll(b, 4, 0))
-            hi = jnp.where(top, pltpu.roll(a, 4, 0), b)
-            out3 = []
-            for xl in range(2):
-                for isk in range(2):
-                    at = 32 * xl + 16 * isk
-                    out = jnp.where(
-                        l8 < 16, roll(m, (128 - at) % 128),
-                        jnp.where(l8 < 32, roll(hi, (16 - 64 - at) % 128), roll(lo, (112 - 64 - at) % 128)),
-                    )
-                    out = jnp.where(in3, out, 0.0)
-                    plane = 1 + 2 * sx + xl
-                    if isk:
-                        out3.append((L3.K, (plane, slice(8 + 8 * q, 16 + 8 * q)), out))
-                    else:
-                        out3.append((L3.R, (plane, slice(8 * q, 8 * q + 8)), out))
-            return out3
-
-        loop(0, 4, 4, load3)
-    L3.build()
-    L3.step(L3.VA, L3.VB, A1, B1, 0, True)
-
-    def residue(i):
-        _, av = L3.flux(L3.VB, i)
-        return [(RES, i - 1, L3.R[i] - av)]
-
-    loop(1, 9, 4, residue)
-    in4 = mask4(0)
-
-    def down4(x):
-        t = (RES[2 * x, pl.ds(0, 16, stride=2)] + RES[2 * x, pl.ds(1, 16, stride=2)]) + (
-            RES[2 * x + 1, pl.ds(0, 16, stride=2)] + RES[2 * x + 1, pl.ds(1, 16, stride=2)]
-        )
-        r4 = jnp.where(in4, pair(t, 16), 0.0)
-        t = (L3.K[1 + 2 * x, pl.ds(8, 16, stride=2)] + L3.K[1 + 2 * x, pl.ds(9, 16, stride=2)]) + (
-            L3.K[2 + 2 * x, pl.ds(8, 16, stride=2)] + L3.K[2 + 2 * x, pl.ds(9, 16, stride=2)]
-        )
-        k4 = jnp.where(in4, 0.125 * pair(t, 16), 0.0)
-        return [(L4.R, 1 + x, r4), (L4.K, (1 + x, slice(8, 24)), k4)]
-
-    loop(0, 4, 4, down4)
-    L4.build()
-    L4.step(L4.VA, L4.VB, A1, B1, 0, True)
-    L4.step(L4.VB, L4.VA, A2, B2, 0)
-    L4.step(L4.VA, L4.VB, A3, B3, 0)
-
-    def repeat_lanes(x, rows):
-        l = lanes(rows)
-        return gat(x, jnp.where(l < 96, l >> 1, (l >> 1) + 64))
-
-    def repeat_rows(ref, slot, x, rows):
-        ref[slot, pl.ds(0, rows, stride=2)] = x
-        ref[slot, pl.ds(1, rows, stride=2)] = x
-        return ref[slot, 0 : 2 * rows]
-
-    def up4(x):
-        t = repeat_rows(T, x, repeat_lanes(L4.VB[1 + x, 8:24], 16), 16)
-        rows = slice(8, 40)
-        return [(L3.VB, (1 + 2 * x + p, rows), L3.VB[1 + 2 * x + p, rows] + t) for p in range(2)]
-
-    loop(0, 4, 4, up4)
-    L3.step(L3.VB, L3.VA, 0.0, B0, 0)
-    L3.step(L3.VA, L3.VB, A1, B1, 0)
-
-    def load2(i):
-        xg = 4 * gx + i - 7 + 8
-        sx = (xg >> 2) - 2
-        xl = xg & 3
-        scx = jnp.clip(sx, 0, 3)
-        m = mask2(i)
-        out2 = []
-        for n in range(3):
-            sy = jnp.clip(gy + n - 1, 0, 7)
-            r, k, edge = E23[sy, scx, 0], E23[sy, scx, 1], E23[sy, scx, 2]
-            mn = m[8 * n : 8 * n + 8]
-            for isk, mid in ((0, r), (1, k)):
-                at = 8 * xl + 32 * isk
-                out = jnp.where(
-                    l8 < 32, roll(mid, (128 - 32 * xl) & 127),
-                    jnp.where(l8 < 64, roll(edge, (224 - at) & 127), roll(edge, (248 - at) & 127)),
-                )
-                out = jnp.where(mn, out, 0.0)
-                if isk:
-                    out2.append((L2.K, (i, slice(8 + 8 * n, 16 + 8 * n)), out))
-                else:
-                    out2.append((L2.R, (i, slice(8 * n, 8 * n + 8)), out))
-        return out2
-
-    loop(0, 18, 6, load2)
-    L2.build()
-    L2.smooth6()
-
-    def up3(q):
-        w = L3.VB[2 * gx + q, pl.ds(4 * gy + 4, 16)]
-        t = repeat_rows(T, 4 + q, repeat_lanes(w, 16), 16)[0:24]
-        rows = slice(8, 32)
-        return [(L2.VB, (2 * q + 5 + p, rows), L2.VB[2 * q + 5 + p, rows] + t) for p in range(2)]
-
-    loop(0, 4, 4, up3)
-
-    def up2(q):
-        t = repeat_rows(T, 8 + q, repeat_lanes(L2.VB[q + 6, 12:28], 16), 16)
-        rows = slice(8, 40)
-        return [(L1.VB, (2 * q + 5 + p, rows), L1.VB[2 * q + 5 + p, rows] + t) for p in range(2)]
-
-    loop(0, 6, 6, up2)
 
     for _, okr, c in cx0:
         each(okr, [c], "wait_recv")
@@ -636,6 +531,119 @@
     ghosts(LS.VA)
     LS.smooth6(after=ghosts, trim=False)
 
+    each_y("wait_recv", True)
+    in3 = yz(8, 0, 8, 16, 16, 16)
+    for sx in range(4):
+        def load3(q, sx=sx):
+            a, b = E23[2 * q, sx, 3], E23[2 * q + 1, sx, 3]
+            m = jnp.where(top, a, b)
+            lo = jnp.where(top, a, pltpu.roll(b, 4, 0))
+            hi = jnp.where(top, pltpu.roll(a, 4, 0), b)
+            out3 = []
+            for xl in range(2):
+                for isk in range(2):
+                    at = 32 * xl + 16 * isk
+                    out = jnp.where(
+                        l8 < 16, roll(m, (128 - at) % 128),
+                        jnp.where(l8 < 32, roll(hi, (16 - 64 - at) % 128), roll(lo, (112 - 64 - at) % 128)),
+                    )
+                    out = jnp.where(in3, out, 0.0)
+                    plane = 1 + 2 * sx + xl
+                    if isk:
+                        out3.append((L3.K, (plane, slice(8 + 8 * q, 16 + 8 * q)), out))
+                    else:
+                        out3.append((L3.R, (plane, slice(8 * q, 8 * q + 8)), out))
+            return out3
+
+        loop(0, 4, 4, load3)
+    L3.build()
+    L3.step(L3.VA, L3.VB, A1, B1, 0, True)
+
+    def residue(i):
+        _, av = L3.flux(L3.VB, i)
+        return [(RES, i - 1, L3.R[i] - av)]
+
+    loop(1, 9, 4, residue)
+    in4 = mask4(0)
+
+    def down4(x):
+        t = (RES[2 * x, pl.ds(0, 16, stride=2)] + RES[2 * x, pl.ds(1, 16, stride=2)]) + (
+            RES[2 * x + 1, pl.ds(0, 16, stride=2)] + RES[2 * x + 1, pl.ds(1, 16, stride=2)]
+        )
+        r4 = jnp.where(in4, pair(t, 16), 0.0)
+        t = (L3.K[1 + 2 * x, pl.ds(8, 16, stride=2)] + L3.K[1 + 2 * x, pl.ds(9, 16, stride=2)]) + (
+            L3.K[2 + 2 * x, pl.ds(8, 16, stride=2)] + L3.K[2 + 2 * x, pl.ds(9, 16, stride=2)]
+        )
+        k4 = jnp.where(in4, 0.125 * pair(t, 16), 0.0)
+        return [(L4.R, 1 + x, r4), (L4.K, (1 + x, slice(8, 24)), k4)]
+
+    loop(0, 4, 4, down4)
+    L4.build()
+    L4.step(L4.VA, L4.VB, A1, B1, 0, True)
+    L4.step(L4.VB, L4.VA, A2, B2, 0)
+    L4.step(L4.VA, L4.VB, A3, B3, 0)
+
+    def repeat_lanes(x, rows):
+        l = lanes(rows)
+        return gat(x, jnp.where(l < 96, l >> 1, (l >> 1) + 64))
+
+    def repeat_rows(ref, slot, x, rows):
+        ref[slot, pl.ds(0, rows, stride=2)] = x
+        ref[slot, pl.ds(1, rows, stride=2)] = x
+        return ref[slot, 0 : 2 * rows]
+
+    def up4(x):
+        t = repeat_rows(T, x, repeat_lanes(L4.VB[1 + x, 8:24], 16), 16)
+        rows = slice(8, 40)
+        return [(L3.VB, (1 + 2 * x + p, rows), L3.VB[1 + 2 * x + p, rows] + t) for p in range(2)]
+
+    loop(0, 4, 4, up4)
+    L3.step(L3.VB, L3.VA, 0.0, B0, 0)
+    L3.step(L3.VA, L3.VB, A1, B1, 0)
+
+    def load2(i):
+        xg = 4 * gx + i - 7 + 8
+        sx = (xg >> 2) - 2
+        xl = xg & 3
+        scx = jnp.clip(sx, 0, 3)
+        m = mask2(i)
+        out2 = []
+        for n in range(3):
+            sy = jnp.clip(gy + n - 1, 0, 7)
+            r, k, edge = E23[sy, scx, 0], E23[sy, scx, 1], E23[sy, scx, 2]
+            mn = m[8 * n : 8 * n + 8]
+            for isk, mid in ((0, r), (1, k)):
+                at = 8 * xl + 32 * isk
+                out = jnp.where(
+                    l8 < 32, roll(mid, (128 - 32 * xl) & 127),
+                    jnp.where(l8 < 64, roll(edge, (224 - at) & 127), roll(edge, (248 - at) & 127)),
+                )
+                out = jnp.where(mn, out, 0.0)
+                if isk:
+                    out2.append((L2.K, (i, slice(8 + 8 * n, 16 + 8 * n)), out))
+                else:
+                    out2.append((L2.R, (i, slice(8 * n, 8 * n + 8)), out))
+        return out2
+
+    loop(0, 18, 6, load2)
+    L2.build()
+    L2.smooth6()
+
+    def up3(q):
+        w = L3.VB[2 * gx + q, pl.ds(4 * gy + 4, 16)]
+        t = repeat_rows(T, 4 + q, repeat_lanes(w, 16), 16)[0:24]
+        rows = slice(8, 32)
+        return [(L2.VB, (2 * q + 5 + p, rows), L2.VB[2 * q + 5 + p, rows] + t) for p in range(2)]
+
+    loop(0, 4, 4, up3)
+
+    def up2(q):
+        t = repeat_rows(T, 8 + q, repeat_lanes(L2.VB[q + 6, 12:28], 16), 16)
+        rows = slice(8, 40)
+        return [(L1.VB, (2 * q + 5 + p, rows), L1.VB[2 * q + 5 + p, rows] + t) for p in range(2)]
+
+    loop(0, 6, 6, up2)
+
     l48, l24 = lanes(48), lanes(24)
 
     def merge(q):
@@ -681,7 +689,7 @@
 
     each(gz > 0, zdown, "wait_send")
     each(gz < 7, zup, "wait_send")
-    for ok, _, c in c0 + c1 + cx0 + cx1:
+    for ok, _, c in c0r + c0k + c1 + cx0 + cx1:
         each(ok, [c], "wait_send")
     for c in gather_x:
         c.wait_send()
@@ -700,7 +708,7 @@
     scratch = [
         vm(2, 30, 48, 128), vm(22, 32, 128), vm(8, 4, 4, 8, 128), vm(3, 2, 3, 48, 128), vm(2, 3, 32, 128),
         vm(4, 8, 128), vm(2, 8, 128), vm(24, 48, 128), vm(10, 48, 128), vm(8, 32, 128), vm(30, 48, 128), vm(30, 48, 128),
-        dma((2,)), dma((8,)), dma((8,)), dma((8,)), dma((8,)), dma((3,)), dma((3,)), dma((2, 4)), dma((2, 4)),
+        dma((2,)), dma((16,)), dma((16,)), dma((8,)), dma((8,)), dma((3,)), dma((3,)), dma((2, 4)), dma((2, 4)),
         dma((16,)), dma((16,)), dma((7,)), dma((7,)),
     ]
     for X, Y in ((30, 48), (12, 48), (22, 32), (18, 24), (10, 32), (6, 16)):

time: 40.2 us -> 38.4 us (0.955)
  Pallas kernels: 35.8 us -> 34.3 us
    pallas_call x1, Pallas kernels: 35.8 us -> 34.3 us  [shards(): pl.pallas_call(kernel, out_shape=(out, out), in_specs=[pl.BlockSpec(memor...]
where the time goes in v5:
time: 38.4 us; the launch traced here: 38.2 us
  Pallas kernels  34.3 us (89%)
  local copies, waits for them, and re-layouts  3.3 us (9%)
  between operations  0.65 us (2%)
    pallas_call x1, Pallas kernels, shards(): pl.pallas_call(kernel, out_shape=(out, out), in_specs=[pl.BlockSpec(memor...  34.3 us
    unnamed x6, local copies, waits for them, and re-layouts  3.3 us

profile of v5, /device:TPU:1, one launch (start us, length us, event | category | flops | bytes accessed | tf_op | source)
XLA Modules:
  0.0 38.2 jit_solution(14588097583448701264)
XLA Ops:
  0.6 0.0 copy-start
  0.6 0.9 %copy-done = f32[16,32,128]{2,1,0:T(8,128)S(1)} copy-done((f32[16,32,128]{2,1,0:T(8,128)S(1)}, f32[16,32,128]{2,1,0:T(8,128)}, u32[]{:S(2)}) %copy-start) | copy-done | bytes 262168
  1.6 0.0 copy-start.1
  1.6 0.9 %copy-done.1 = f32[16,32,128]{2,1,0:T(8,128)S(1)} copy-done((f32[16,32,128]{2,1,0:T(8,128)S(1)}, f32[16,32,128]{2,1,0:T(8,128)}, u32[]{:S(2)}) %copy-start.1) | copy-done | bytes 262168
  2.5 34.3 %multigrid.1 = (f32[16,32,128]{2,1,0:T(8,128)S(1)}, f32[16,32,128]{2,1,0:T(8,128)S(1)}) custom-call(f32[16,32,128]{2,1,0:T(8,128)S(1)} %copy-done, f32[16,32,128]{2,1,0:T(8,128)S(1)} %copy-done.1), custom_call_target="tpu_custom_call" | custom-call | tf_op jit(solution)/shard_map/multigrid/pallas_call | solution.py:716
  36.8 0.7 %copy.6 = f32[16,32,128]{2,1,0:T(8,128)} copy(f32[16,32,128]{2,1,0:T(8,128)S(1)} %get-tuple-element.4) | data formatting | bytes 524288
  37.5 0.7 %copy.7 = f32[16,32,128]{2,1,0:T(8,128)} copy(f32[16,32,128]{2,1,0:T(8,128)S(1)} %get-tuple-element.5) | data formatting | bytes 524288
Async XLA Ops:
  0.6 1.0 %copy-start = (f32[16,32,128]{2,1,0:T(8,128)S(1)}, f32[16,32,128]{2,1,0:T(8,128)}, u32[]{:S(2)}) copy-start(f32[16,32,128]{2,1,0:T(8,128)} %r_in.1) | copy-start | bytes 786436
  1.6 0.9 %copy-start.1 = (f32[16,32,128]{2,1,0:T(8,128)S(1)}, f32[16,32,128]{2,1,0:T(8,128)}, u32[]{:S(2)}) copy-start(f32[16,32,128]{2,1,0:T(8,128)} %k_in.1) | copy-start | bytes 786436

commit v6 on v5

--- a/solution.py
+++ b/solution.py
@@ -369,9 +369,14 @@
             return sl(pairs)
         return sl((pairs[0] + 1, pairs[1])) if dx == 1 else sl((pairs[0], pairs[1] - 1))
 
+    def planes(pairs, dx, dy, arr):
+        cut = (abs(dx) if arr == 0 else 0) + abs(dx * dy)
+        return sl((pairs[0] + cut, pairs[1])) if dx == 1 else sl((pairs[0], pairs[1] - cut))
+
     def fine(arr):
         return near_copies(lambda n, dx, dy: rc(
-            E0.at[arr, thinner(SRC0X[dx], dx, dy), sl(SRC0Y[dy])], E0.at[arr, thinner(DST0X[dx], dx, dy), sl(DST0Y[dy])],
+            E0.at[arr, planes(SRC0X[dx], dx, dy, arr), sl(SRC0Y[dy])],
+            E0.at[arr, planes(DST0X[dx], dx, dy, arr), sl(DST0Y[dy])],
             e0s.at[8 * arr + n], e0r.at[8 * arr + n], dev_near(dx, dy)))
 
     c0r, c0k = fine(0), fine(1)

time: 38.4 us -> 38.3 us (level)
  no operation moved by 1% of the time
where the time goes in v6:
time: 38.3 us; the launch traced here: 38.2 us
  Pallas kernels  34.2 us (89%)
  local copies, waits for them, and re-layouts  3.3 us (9%)
  between operations  0.65 us (2%)
    pallas_call x1, Pallas kernels, shards(): pl.pallas_call(kernel, out_shape=(out, out), in_specs=[pl.BlockSpec(memor...  34.2 us
    unnamed x6, local copies, waits for them, and re-layouts  3.3 us

profile of v6, /device:TPU:1, one launch (start us, length us, event | category | flops | bytes accessed | tf_op | source)
XLA Modules:
  0.0 38.2 jit_solution(16121517222340469991)
XLA Ops:
  0.6 0.0 copy-start
  0.6 0.9 %copy-done = f32[16,32,128]{2,1,0:T(8,128)S(1)} copy-done((f32[16,32,128]{2,1,0:T(8,128)S(1)}, f32[16,32,128]{2,1,0:T(8,128)}, u32[]{:S(2)}) %copy-start) | copy-done | bytes 262168
  1.6 0.0 copy-start.1
  1.6 0.9 %copy-done.1 = f32[16,32,128]{2,1,0:T(8,128)S(1)} copy-done((f32[16,32,128]{2,1,0:T(8,128)S(1)}, f32[16,32,128]{2,1,0:T(8,128)}, u32[]{:S(2)}) %copy-start.1) | copy-done | bytes 262168
  2.5 34.2 %multigrid.1 = (f32[16,32,128]{2,1,0:T(8,128)S(1)}, f32[16,32,128]{2,1,0:T(8,128)S(1)}) custom-call(f32[16,32,128]{2,1,0:T(8,128)S(1)} %copy-done, f32[16,32,128]{2,1,0:T(8,128)S(1)} %copy-done.1), custom_call_target="tpu_custom_call" | custom-call | tf_op jit(solution)/shard_map/multigrid/pallas_call | solution.py:721
  36.8 0.7 %copy.6 = f32[16,32,128]{2,1,0:T(8,128)} copy(f32[16,32,128]{2,1,0:T(8,128)S(1)} %get-tuple-element.4) | data formatting | bytes 524288
  37.5 0.7 %copy.7 = f32[16,32,128]{2,1,0:T(8,128)} copy(f32[16,32,128]{2,1,0:T(8,128)S(1)} %get-tuple-element.5) | data formatting | bytes 524288
Async XLA Ops:
  0.6 1.0 %copy-start = (f32[16,32,128]{2,1,0:T(8,128)S(1)}, f32[16,32,128]{2,1,0:T(8,128)}, u32[]{:S(2)}) copy-start(f32[16,32,128]{2,1,0:T(8,128)} %r_in.1) | copy-start | bytes 786436
  1.6 0.9 %copy-start.1 = (f32[16,32,128]{2,1,0:T(8,128)S(1)}, f32[16,32,128]{2,1,0:T(8,128)}, u32[]{:S(2)}) copy-start(f32[16,32,128]{2,1,0:T(8,128)} %k_in.1) | copy-start | bytes 786436
